TPU v7x, 32 devices: a whole 2x2x4 slice. The times are simulated.
32 devices in a mesh: tm: 8 (over y, x, core), row: 4 (over z).
Axes of the slice: x: 2, y: 2, z: 4, core: 2. Of those that a mesh axis runs over, the one named last changes fastest.
Arguments:
- right_side: float32 [8, 256, 1024], P('tm', 'row'), may hold values from -6 to 6
- kappa: float32 [256, 1024], P('row'), may hold values from 0.5 to 8
Outputs:
- solution: float32 [8, 256, 1024], P('tm', 'row')
All inputs are finite; a program needn't handle non-finite values.
Results may differ from a plain program's by a relative error of at most 0.0003.
Values sent between devices are 32-bit elements; how exact they have to be, the bound alone decides.
A program may use at most 64 MiB of HBM per device.

v0:
```python
import math

import jax
import jax.numpy as jnp
from jax import lax
from jax.sharding import PartitionSpec as P

SWEEPS = 2
DEGREE = 4


circulant_alpha = 0.05
courant_rows = 0.5
courant_cols = 0.25
cheb_centre = 1.0
cheb_half = 0.7


def from_partner(value, axis, bit):
    mask = 2**bit
    pairs = [(source, source ^ mask) for source in range(lax.axis_size(axis))]
    return lax.ppermute(value, axis, pairs)


def padded_2(block, sides, width):
    for axis, dim in sides:
        count = lax.axis_size(axis)
        forward = [(i, i + 1) for i in range(count - 1)]
        backward = [(target, source) for source, target in forward]
        low = lax.ppermute(
            lax.slice_in_dim(block, block.shape[dim] - width, None, axis=dim), axis, forward
        )
        high = lax.ppermute(lax.slice_in_dim(block, 0, width, axis=dim), axis, backward)
        block = jnp.concatenate([low, block, high], axis=dim)
    return block


def step_weights(count):
    return [
        1.0 / (cheb_centre + cheb_half * math.cos(math.pi * (2 * number + 1) / (2 * count)))
        for number in range(count)
    ]


def face_terms(kappa_rows):
    padded = jnp.pad(kappa_rows, ((0, 0), (1, 1)))
    centre = padded[1:-1, 1:-1]
    north = 0.5 * (centre + padded[2:, 1:-1])
    south = 0.5 * (centre + padded[:-2, 1:-1])
    east = 0.5 * (centre + padded[1:-1, 2:])
    west = 0.5 * (centre + padded[1:-1, :-2])
    diagonal = north + south + east + west + (courant_rows + courant_cols)
    return (north, south, east, west, diagonal)


def spatial(extended, faces):
    north, south, east, west, diagonal = faces
    padded = jnp.pad(extended, ((0, 0), (0, 0), (0, 0), (1, 1)))
    centre = padded[:, :, 1:-1, 1:-1]
    above = padded[:, :, 2:, 1:-1]
    below = padded[:, :, :-2, 1:-1]
    after = padded[:, :, 1:-1, 2:]
    before = padded[:, :, 1:-1, :-2]
    coupled = north * above + south * below + east * after + west * before
    return diagonal * centre - coupled - courant_rows * below - courant_cols * before


def rotate(pair, cosine, sine):
    return jnp.stack([pair[0] * cosine - pair[1] * sine, pair[0] * sine + pair[1] * cosine])


def short_transform(pair, sign):
    count = pair.shape[1]
    index = jnp.arange(count, dtype=jnp.int32)
    angles = 2.0 * math.pi / count * (index[:, None] * index[None, :] % count).astype(jnp.float32)
    cosine = jnp.cos(angles)
    sine = sign * jnp.sin(angles)
    highest = lax.Precision.HIGHEST
    real = jnp.einsum("kj,jrc->krc", cosine, pair[0], precision=highest) - jnp.einsum(
        "kj,jrc->krc", sine, pair[1], precision=highest
    )
    imag = jnp.einsum("kj,jrc->krc", cosine, pair[1], precision=highest) + jnp.einsum(
        "kj,jrc->krc", sine, pair[0], precision=highest
    )
    return jnp.stack([real, imag])


def bit_reversed(device, levels):
    total = jnp.zeros((), jnp.int32)
    for place in range(levels):
        total = total + device // 2**place % 2 * 2 ** (levels - 1 - place)
    return total


def forward_pairs(scaled, device, levels, tm_size, total_steps):
    place = levels - 1
    half = 2**place
    lower = device // half % 2 == 1
    angle = -math.pi / half * (device % half).astype(jnp.float32)
    partner = from_partner(scaled, "tm", place)
    summed = scaled + partner
    differ = partner - scaled
    real = jnp.where(lower, differ * jnp.cos(angle), summed)
    imag = jnp.where(lower, differ * jnp.sin(angle), jnp.zeros_like(summed))
    state = jnp.stack([real, imag])
    for place in range(levels - 2, -1, -1):
        half = 2**place
        lower = device // half % 2 == 1
        angle = -math.pi / half * (device % half).astype(jnp.float32)
        partner = from_partner(state, "tm", place)
        summed = state + partner
        rotated = rotate(partner - state, jnp.cos(angle), jnp.sin(angle))
        state = jnp.where(lower, rotated, summed)
    first_index = bit_reversed(device, levels)
    steps_dev = scaled.shape[0]
    local_steps = jnp.arange(steps_dev, dtype=jnp.int32)
    twist = (
        -2.0 * math.pi / total_steps * (local_steps * first_index % total_steps).astype(jnp.float32)
    )
    state = rotate(state, jnp.cos(twist)[:, None, None], jnp.sin(twist)[:, None, None])
    spectrum = short_transform(state, -1.0)
    frequencies = first_index + tm_size * local_steps
    return (spectrum, frequencies)


def backward_pairs(solved, device, levels, total_steps):
    steps_dev = solved.shape[1]
    first_index = bit_reversed(device, levels)
    state = short_transform(solved, 1.0) * (1.0 / steps_dev)
    local_steps = jnp.arange(steps_dev, dtype=jnp.int32)
    twist = (
        2.0 * math.pi / total_steps * (local_steps * first_index % total_steps).astype(jnp.float32)
    )
    state = rotate(state, jnp.cos(twist)[:, None, None], jnp.sin(twist)[:, None, None])
    for place in range(0, levels - 1):
        half = 2**place
        lower = device // half % 2 == 1
        angle = math.pi / half * (device % half).astype(jnp.float32)
        cosine = jnp.cos(angle)
        sine = jnp.sin(angle)
        partner = from_partner(state, "tm", place)
        upper_value = (state + rotate(partner, cosine, sine)) * 0.5
        lower_value = (partner - rotate(state, cosine, sine)) * 0.5
        state = jnp.where(lower, lower_value, upper_value)
    place = levels - 1
    half = 2**place
    lower = device // half % 2 == 1
    angle = math.pi / half * (device % half).astype(jnp.float32)
    own_turned = state[0] * jnp.cos(angle) - state[1] * jnp.sin(angle)
    outgoing = jnp.where(lower, own_turned, state[0])
    received = from_partner(outgoing, "tm", place)
    return jnp.where(lower, (received - own_turned) * 0.5, (state[0] + received) * 0.5)


def shift_terms(frequencies, faces, total_steps):
    decay = circulant_alpha ** (1.0 / total_steps)
    theta = 2.0 * math.pi / total_steps * frequencies.astype(jnp.float32)
    shift_real = (1.0 - decay * jnp.cos(theta))[:, None, None]
    shift_imag = (decay * jnp.sin(theta))[:, None, None]
    diag_real = shift_real + faces[4]
    magnitude = diag_real * diag_real + shift_imag * shift_imag
    return (shift_real, shift_imag, diag_real / magnitude, -shift_imag / magnitude)


def solve_each(spectrum, frequencies, kappa):
    total_steps = spectrum.shape[1] * lax.axis_size("tm")
    kappa_rows = padded_2(kappa, (("row", 0),), 1)
    faces = face_terms(kappa_rows)
    shift_real, shift_imag, inv_real, inv_imag = shift_terms(frequencies, faces, total_steps)
    state = jnp.zeros_like(spectrum)
    first = True
    for sweep in range(SWEEPS):
        for weight in step_weights(DEGREE):
            if first:
                residual = spectrum
                first = False
            else:
                extended = padded_2(state, (("row", 2),), 1)
                image = spatial(extended, faces)
                image_real = shift_real * state[0] - shift_imag * state[1] + image[0]
                image_imag = shift_real * state[1] + shift_imag * state[0] + image[1]
                residual = spectrum - jnp.stack([image_real, image_imag])
            corr_real = inv_real * residual[0] - inv_imag * residual[1]
            corr_imag = inv_real * residual[1] + inv_imag * residual[0]
            state = state + weight * jnp.stack([corr_real, corr_imag])
    return state


def solve_block(spectrum, frequencies, kappa):
    return solve_each(spectrum, frequencies, kappa)


def body(right_side, kappa):
    steps_dev = right_side.shape[0]
    tm_size = lax.axis_size("tm")
    total_steps = steps_dev * tm_size
    device = lax.axis_index("tm")
    local_steps = jnp.arange(steps_dev, dtype=jnp.int32)
    global_steps = device * steps_dev + local_steps
    log_alpha = math.log(circulant_alpha)
    step_float = global_steps.astype(jnp.float32)
    scaled = right_side * jnp.exp(log_alpha * step_float / total_steps)[:, None, None]
    levels = tm_size.bit_length() - 1
    spectrum, frequencies = forward_pairs(scaled, device, levels, tm_size, total_steps)
    solved = solve_block(spectrum, frequencies, kappa)
    signal = backward_pairs(solved, device, levels, total_steps)
    return signal * jnp.exp(-log_alpha * step_float / total_steps)[:, None, None]


def solution(mesh):
    placed = (P("tm", "row", None), P("row", None))
    return jax.shard_map(
        body, mesh=mesh, in_specs=placed, out_specs=P("tm", "row", None), check_vma=False
    )
```

profile of v0, /device:TPU:0, one launch (start us, length us, event | category | flops | bytes accessed | tf_op | source)
XLA Modules:
  0.0 121.7 jit_solution(8800071670619412570)
XLA Ops:
  1.1 3.0 %collective-permute-start.2 = (f32[1,64,1024]{2,1,0:T(8,128)S(1)}, f32[1,64,1024]{2,1,0:T(8,128)S(1)}, u32[]{:S(2)}, u32[]{:S(2)}) collective-permute-start(f32[1,64,1024]{2,1,0:T(8,128)S(1)} %broadcast_multiply_fusion), channel_id=1, source_target_pairs={{0,16},{4,20},{8,24},{12,28},{16,0},{20,4},{24,8},{28,12},{1,17},{... | collective-permute-start | bytes 786440 | tf_op jit(solution)/shard_map/ppermute | solution.py:22
  4.3 6.1 %collective-permute-done.2 = f32[1,64,1024]{2,1,0:T(8,128)S(1)} collective-permute-done((f32[1,64,1024]{2,1,0:T(8,128)S(1)}, f32[1,64,1024]{2,1,0:T(8,128)S(1)}, u32[]{:S(2)}, u32[]{:S(2)}) %collective-permute-start.2) | collective-permute-done | bytes 262176 | tf_op jit(solution)/shard_map/ppermute | solution.py:22
  10.6 1.8 %collective-permute-start.3 = (f32[2,1,64,1024]{3,2,1,0:T(8,128)S(1)}, f32[2,1,64,1024]{3,2,1,0:T(8,128)S(1)}, u32[]{:S(2)}, u32[]{:S(2)}) collective-permute-start(f32[2,1,64,1024]{3,2,1,0:T(8,128)S(1)} %pad_maximum_fusion.14), channel_id=1, source_target_pairs={{0,8},{4,12},{8,0},{12,4},{16,24},{20,28},{24,16},{28,20},{1,9},{5... | collective-permute-start | bytes 1572872 | tf_op jit(solution)/shard_map/ppermute | solution.py:22
  12.5 11.2 %collective-permute-done.3 = f32[2,1,64,1024]{3,2,1,0:T(8,128)S(1)} collective-permute-done((f32[2,1,64,1024]{3,2,1,0:T(8,128)S(1)}, f32[2,1,64,1024]{3,2,1,0:T(8,128)S(1)}, u32[]{:S(2)}, u32[]{:S(2)}) %collective-permute-start.3) | collective-permute-done | bytes 524320 | tf_op jit(solution)/shard_map/ppermute | solution.py:22
  26.1 4.5 %collective-permute-start.1 = (f32[1,1024]{1,0:T(1,128)S(1)}, f32[1,1024]{1,0:T(1,128)S(1)}, u32[]{:S(2)}, u32[]{:S(2)}) collective-permute-start(f32[1,1024]{1,0:T(1,128)S(1)} %get-tuple-element.76), channel_id=1, source_target_pairs={{0,1},{1,2},{2,3},{4,5},{5,6},{6,7},{8,9},{9,10},{10,11},{12,13},{... | collective-permute-start | bytes 12296 | tf_op jit(solution)/shard_map/ppermute | solution.py:30
  34.6 4.8 %collective-permute-start.6 = (f32[2,1,1,1024]{3,2,1,0:T(1,128)S(1)}, f32[2,1,1,1024]{3,2,1,0:T(1,128)S(1)}, u32[]{:S(2)}, u32[]{:S(2)}) collective-permute-start(f32[2,1,1,1024]{3,2,1,0:T(1,128)S(1)} %get-tuple-element.68), channel_id=1, source_target_pairs={{0,1},{1,2},{2,3},{4,5},{5,6},{6,7},{8,9},{9,10},{10,11},{12,13},{... | collective-permute-start | bytes 24584 | tf_op jit(solution)/shard_map/ppermute | solution.py:30
  39.4 1.3 %collective-permute-done.6 = f32[2,1,1,1024]{3,2,1,0:T(1,128)S(1)} collective-permute-done((f32[2,1,1,1024]{3,2,1,0:T(1,128)S(1)}, f32[2,1,1,1024]{3,2,1,0:T(1,128)S(1)}, u32[]{:S(2)}, u32[]{:S(2)}) %collective-permute-start.6) | collective-permute-done | bytes 8224 | tf_op jit(solution)/shard_map/ppermute | solution.py:30
  43.1 4.8 %collective-permute-start.8 = (f32[2,1,1,1024]{3,2,1,0:T(1,128)S(1)}, f32[2,1,1,1024]{3,2,1,0:T(1,128)S(1)}, u32[]{:S(2)}, u32[]{:S(2)}) collective-permute-start(f32[2,1,1,1024]{3,2,1,0:T(1,128)S(1)} %get-tuple-element.62), channel_id=1, source_target_pairs={{0,1},{1,2},{2,3},{4,5},{5,6},{6,7},{8,9},{9,10},{10,11},{12,13},{... | collective-permute-start | bytes 24584 | tf_op jit(solution)/shard_map/ppermute | solution.py:30
  48.0 1.3 %collective-permute-done.8 = f32[2,1,1,1024]{3,2,1,0:T(1,128)S(1)} collective-permute-done((f32[2,1,1,1024]{3,2,1,0:T(1,128)S(1)}, f32[2,1,1,1024]{3,2,1,0:T(1,128)S(1)}, u32[]{:S(2)}, u32[]{:S(2)}) %collective-permute-start.8) | collective-permute-done | bytes 8224 | tf_op jit(solution)/shard_map/ppermute | solution.py:30
  50.5 4.2 %collective-permute-start.10 = (f32[2,1,1,1024]{3,2,1,0:T(1,128)S(1)}, f32[2,1,1,1024]{3,2,1,0:T(1,128)S(1)}, u32[]{:S(2)}, u32[]{:S(2)}) collective-permute-start(f32[2,1,1,1024]{3,2,1,0:T(1,128)S(1)} %get-tuple-element.60), channel_id=1, source_target_pairs={{0,1},{1,2},{2,3},{4,5},{5,6},{6,7},{8,9},{9,10},{10,11},{12,13},{... | collective-permute-start | bytes 24584 | tf_op jit(solution)/shard_map/ppermute | solution.py:30
  54.7 1.3 %collective-permute-start.9 = (f32[2,1,1,1024]{3,2,1,0:T(1,128)S(1)}, f32[2,1,1,1024]{3,2,1,0:T(1,128)S(1)}, u32[]{:S(2)}, u32[]{:S(2)}) collective-permute-start(f32[2,1,1,1024]{3,2,1,0:T(1,128)S(1)} %get-tuple-element.61), channel_id=1, source_target_pairs={{1,0},{2,1},{3,2},{5,4},{6,5},{7,6},{9,8},{10,9},{11,10},{13,12},{... | collective-permute-start | bytes 24584 | tf_op jit(solution)/shard_map/ppermute | solution.py:33
  56.0 4.2 %collective-permute-done.9 = f32[2,1,1,1024]{3,2,1,0:T(1,128)S(1)} collective-permute-done((f32[2,1,1,1024]{3,2,1,0:T(1,128)S(1)}, f32[2,1,1,1024]{3,2,1,0:T(1,128)S(1)}, u32[]{:S(2)}, u32[]{:S(2)}) %collective-permute-start.9) | collective-permute-done | bytes 8224 | tf_op jit(solution)/shard_map/ppermute | solution.py:33
  62.7 4.5 %collective-permute-start.12 = (f32[2,1,1,1024]{3,2,1,0:T(1,128)S(1)}, f32[2,1,1,1024]{3,2,1,0:T(1,128)S(1)}, u32[]{:S(2)}, u32[]{:S(2)}) collective-permute-start(f32[2,1,1,1024]{3,2,1,0:T(1,128)S(1)} %get-tuple-element.58), channel_id=1, source_target_pairs={{0,1},{1,2},{2,3},{4,5},{5,6},{6,7},{8,9},{9,10},{10,11},{12,13},{... | collective-permute-start | bytes 24584 | tf_op jit(solution)/shard_map/ppermute | solution.py:30
  67.3 1.3 %collective-permute-done.12 = f32[2,1,1,1024]{3,2,1,0:T(1,128)S(1)} collective-permute-done((f32[2,1,1,1024]{3,2,1,0:T(1,128)S(1)}, f32[2,1,1,1024]{3,2,1,0:T(1,128)S(1)}, u32[]{:S(2)}, u32[]{:S(2)}) %collective-permute-start.12) | collective-permute-done | bytes 8224 | tf_op jit(solution)/shard_map/ppermute | solution.py:30
  71.2 4.8 %collective-permute-start.14 = (f32[2,1,1,1024]{3,2,1,0:T(1,128)S(1)}, f32[2,1,1,1024]{3,2,1,0:T(1,128)S(1)}, u32[]{:S(2)}, u32[]{:S(2)}) collective-permute-start(f32[2,1,1,1024]{3,2,1,0:T(1,128)S(1)} %get-tuple-element.56), channel_id=1, source_target_pairs={{0,1},{1,2},{2,3},{4,5},{5,6},{6,7},{8,9},{9,10},{10,11},{12,13},{... | collective-permute-start | bytes 24584 | tf_op jit(solution)/shard_map/ppermute | solution.py:30
  76.0 1.3 %collective-permute-done.14 = f32[2,1,1,1024]{3,2,1,0:T(1,128)S(1)} collective-permute-done((f32[2,1,1,1024]{3,2,1,0:T(1,128)S(1)}, f32[2,1,1,1024]{3,2,1,0:T(1,128)S(1)}, u32[]{:S(2)}, u32[]{:S(2)}) %collective-permute-start.14) | collective-permute-done | bytes 8224 | tf_op jit(solution)/shard_map/ppermute | solution.py:30
  79.9 4.8 %collective-permute-start.16 = (f32[2,1,1,1024]{3,2,1,0:T(1,128)S(1)}, f32[2,1,1,1024]{3,2,1,0:T(1,128)S(1)}, u32[]{:S(2)}, u32[]{:S(2)}) collective-permute-start(f32[2,1,1,1024]{3,2,1,0:T(1,128)S(1)} %get-tuple-element.54), channel_id=1, source_target_pairs={{0,1},{1,2},{2,3},{4,5},{5,6},{6,7},{8,9},{9,10},{10,11},{12,13},{... | collective-permute-start | bytes 24584 | tf_op jit(solution)/shard_map/ppermute | solution.py:30
  84.8 1.3 %collective-permute-done.16 = f32[2,1,1,1024]{3,2,1,0:T(1,128)S(1)} collective-permute-done((f32[2,1,1,1024]{3,2,1,0:T(1,128)S(1)}, f32[2,1,1,1024]{3,2,1,0:T(1,128)S(1)}, u32[]{:S(2)}, u32[]{:S(2)}) %collective-permute-start.16) | collective-permute-done | bytes 8224 | tf_op jit(solution)/shard_map/ppermute | solution.py:30
  88.8 5.0 %collective-permute-start.18 = (f32[2,1,1,1024]{3,2,1,0:T(1,128)S(1)}, f32[2,1,1,1024]{3,2,1,0:T(1,128)S(1)}, u32[]{:S(2)}, u32[]{:S(2)}) collective-permute-start(f32[2,1,1,1024]{3,2,1,0:T(1,128)S(1)} %get-tuple-element.52), channel_id=1, source_target_pairs={{0,1},{1,2},{2,3},{4,5},{5,6},{6,7},{8,9},{9,10},{10,11},{12,13},{... | collective-permute-start | bytes 24584 | tf_op jit(solution)/shard_map/ppermute | solution.py:30
  96.7 1.9 %collective-permute-done.19 = f32[2,1,64,1024]{3,2,1,0:T(8,128)S(1)} collective-permute-done((f32[2,1,64,1024]{3,2,1,0:T(8,128)S(1)}, f32[2,1,64,1024]{3,2,1,0:T(8,128)S(1)}, u32[]{:S(2)}, u32[]{:S(2)}) %collective-permute-start.19) | collective-permute-done | bytes 524320 | tf_op jit(solution)/shard_map/ppermute | solution.py:22
  98.8 1.5 %collective-permute-start.20 = (f32[2,1,64,1024]{3,2,1,0:T(8,128)S(1)}, f32[2,1,64,1024]{3,2,1,0:T(8,128)S(1)}, u32[]{:S(2)}, u32[]{:S(2)}) collective-permute-start(f32[2,1,64,1024]{3,2,1,0:T(8,128)S(1)} %fusion.58), channel_id=1, source_target_pairs={{0,8},{4,12},{8,0},{12,4},{16,24},{20,28},{24,16},{28,20},{1,9},{5... | collective-permute-start | bytes 1572872 | tf_op jit(solution)/shard_map/ppermute | solution.py:22
  100.7 12.2 %collective-permute-done.20 = f32[2,1,64,1024]{3,2,1,0:T(8,128)S(1)} collective-permute-done((f32[2,1,64,1024]{3,2,1,0:T(8,128)S(1)}, f32[2,1,64,1024]{3,2,1,0:T(8,128)S(1)}, u32[]{:S(2)}, u32[]{:S(2)}) %collective-permute-start.20) | collective-permute-done | bytes 524320 | tf_op jit(solution)/shard_map/ppermute | solution.py:22
  113.4 1.5 %collective-permute-start.21 = (f32[1,64,1024]{2,1,0:T(8,128)S(1)}, f32[1,64,1024]{2,1,0:T(8,128)S(1)}, u32[]{:S(2)}, u32[]{:S(2)}) collective-permute-start(f32[1,64,1024]{2,1,0:T(8,128)S(1)} %fusion.74), channel_id=1, source_target_pairs={{0,16},{4,20},{8,24},{12,28},{16,0},{20,4},{24,8},{28,12},{1,17},{... | collective-permute-start | bytes 786440 | tf_op jit(solution)/shard_map/ppermute | solution.py:22
  114.9 6.0 %collective-permute-done.21 = f32[1,64,1024]{2,1,0:T(8,128)S(1)} collective-permute-done((f32[1,64,1024]{2,1,0:T(8,128)S(1)}, f32[1,64,1024]{2,1,0:T(8,128)S(1)}, u32[]{:S(2)}, u32[]{:S(2)}) %collective-permute-start.21) | collective-permute-done | bytes 262176 | tf_op jit(solution)/shard_map/ppermute | solution.py:22
  (97 shorter events, 25.2 us)
Async XLA Ops:
  0.0 10.4 %copy-start.1 = (f32[1,64,1024]{2,1,0:T(8,128)S(1)}, f32[1,64,1024]{2,1,0:T(8,128)}, u32[]{:S(2)}) copy-start(f32[1,64,1024]{2,1,0:T(8,128)} %param.2) | copy-start | bytes 786436
  1.1 9.3 %collective-permute-start.2 = (f32[1,64,1024]{2,1,0:T(8,128)S(1)}, f32[1,64,1024]{2,1,0:T(8,128)S(1)}, u32[]{:S(2)}, u32[]{:S(2)}) collective-permute-start(f32[1,64,1024]{2,1,0:T(8,128)S(1)} %broadcast_multiply_fusion), channel_id=1, source_target_pairs={{0,16},{4,20},{8,24},{12,28},{16,0},{20,4},{24,8},{28,12},{1,17},{... | collective-permute-start | bytes 786440 | tf_op jit(solution)/shard_map/ppermute | solution.py:22
  10.6 13.2 %collective-permute-start.3 = (f32[2,1,64,1024]{3,2,1,0:T(8,128)S(1)}, f32[2,1,64,1024]{3,2,1,0:T(8,128)S(1)}, u32[]{:S(2)}, u32[]{:S(2)}) collective-permute-start(f32[2,1,64,1024]{3,2,1,0:T(8,128)S(1)} %pad_maximum_fusion.14), channel_id=1, source_target_pairs={{0,8},{4,12},{8,0},{12,4},{16,24},{20,28},{24,16},{28,20},{1,9},{5... | collective-permute-start | bytes 1572872 | tf_op jit(solution)/shard_map/ppermute | solution.py:22
  23.9 1.0 copy-start
  24.0 8.4 %collective-permute-start.4 = (f32[2,1,64,1024]{3,2,1,0:T(8,128)S(1)}, f32[2,1,64,1024]{3,2,1,0:T(8,128)S(1)}, u32[]{:S(2)}, u32[]{:S(2)}) collective-permute-start(f32[2,1,64,1024]{3,2,1,0:T(8,128)S(1)} %maximum_select_fusion), channel_id=1, source_target_pairs={{0,4},{4,0},{8,12},{12,8},{16,20},{20,16},{24,28},{28,24},{1,5},{5... | collective-permute-start | bytes 1572872 | tf_op jit(solution)/shard_map/ppermute | solution.py:22
  24.9 6.0 %collective-permute-start = (f32[1,1024]{1,0:T(1,128)S(1)}, f32[1,1024]{1,0:T(1,128)S(1)}, u32[]{:S(2)}, u32[]{:S(2)}) collective-permute-start(f32[1,1024]{1,0:T(1,128)S(1)} %get-tuple-element.77), channel_id=1, source_target_pairs={{1,0},{2,1},{3,2},{5,4},{6,5},{7,6},{9,8},{10,9},{11,10},{13,12},{... | collective-permute-start | bytes 12296 | tf_op jit(solution)/shard_map/ppermute | solution.py:33
  26.1 5.9 %collective-permute-start.1 = (f32[1,1024]{1,0:T(1,128)S(1)}, f32[1,1024]{1,0:T(1,128)S(1)}, u32[]{:S(2)}, u32[]{:S(2)}) collective-permute-start(f32[1,1024]{1,0:T(1,128)S(1)} %get-tuple-element.76), channel_id=1, source_target_pairs={{0,1},{1,2},{2,3},{4,5},{5,6},{6,7},{8,9},{9,10},{10,11},{12,13},{... | collective-permute-start | bytes 12296 | tf_op jit(solution)/shard_map/ppermute | solution.py:30
  33.3 6.1 %collective-permute-start.5 = (f32[2,1,1,1024]{3,2,1,0:T(1,128)S(1)}, f32[2,1,1,1024]{3,2,1,0:T(1,128)S(1)}, u32[]{:S(2)}, u32[]{:S(2)}) collective-permute-start(f32[2,1,1,1024]{3,2,1,0:T(1,128)S(1)} %get-tuple-element.69), channel_id=1, source_target_pairs={{1,0},{2,1},{3,2},{5,4},{6,5},{7,6},{9,8},{10,9},{11,10},{13,12},{... | collective-permute-start | bytes 24584 | tf_op jit(solution)/shard_map/ppermute | solution.py:33
  34.6 6.2 %collective-permute-start.6 = (f32[2,1,1,1024]{3,2,1,0:T(1,128)S(1)}, f32[2,1,1,1024]{3,2,1,0:T(1,128)S(1)}, u32[]{:S(2)}, u32[]{:S(2)}) collective-permute-start(f32[2,1,1,1024]{3,2,1,0:T(1,128)S(1)} %get-tuple-element.68), channel_id=1, source_target_pairs={{0,1},{1,2},{2,3},{4,5},{5,6},{6,7},{8,9},{9,10},{10,11},{12,13},{... | collective-permute-start | bytes 24584 | tf_op jit(solution)/shard_map/ppermute | solution.py:30
  41.8 6.1 %collective-permute-start.7 = (f32[2,1,1,1024]{3,2,1,0:T(1,128)S(1)}, f32[2,1,1,1024]{3,2,1,0:T(1,128)S(1)}, u32[]{:S(2)}, u32[]{:S(2)}) collective-permute-start(f32[2,1,1,1024]{3,2,1,0:T(1,128)S(1)} %get-tuple-element.63), channel_id=1, source_target_pairs={{1,0},{2,1},{3,2},{5,4},{6,5},{7,6},{9,8},{10,9},{11,10},{13,12},{... | collective-permute-start | bytes 24584 | tf_op jit(solution)/shard_map/ppermute | solution.py:33
  43.1 6.2 %collective-permute-start.8 = (f32[2,1,1,1024]{3,2,1,0:T(1,128)S(1)}, f32[2,1,1,1024]{3,2,1,0:T(1,128)S(1)}, u32[]{:S(2)}, u32[]{:S(2)}) collective-permute-start(f32[2,1,1,1024]{3,2,1,0:T(1,128)S(1)} %get-tuple-element.62), channel_id=1, source_target_pairs={{0,1},{1,2},{2,3},{4,5},{5,6},{6,7},{8,9},{9,10},{10,11},{12,13},{... | collective-permute-start | bytes 24584 | tf_op jit(solution)/shard_map/ppermute | solution.py:30
  50.5 5.5 %collective-permute-start.10 = (f32[2,1,1,1024]{3,2,1,0:T(1,128)S(1)}, f32[2,1,1,1024]{3,2,1,0:T(1,128)S(1)}, u32[]{:S(2)}, u32[]{:S(2)}) collective-permute-start(f32[2,1,1,1024]{3,2,1,0:T(1,128)S(1)} %get-tuple-element.60), channel_id=1, source_target_pairs={{0,1},{1,2},{2,3},{4,5},{5,6},{6,7},{8,9},{9,10},{10,11},{12,13},{... | collective-permute-start | bytes 24584 | tf_op jit(solution)/shard_map/ppermute | solution.py:30
  54.7 5.5 %collective-permute-start.9 = (f32[2,1,1,1024]{3,2,1,0:T(1,128)S(1)}, f32[2,1,1,1024]{3,2,1,0:T(1,128)S(1)}, u32[]{:S(2)}, u32[]{:S(2)}) collective-permute-start(f32[2,1,1,1024]{3,2,1,0:T(1,128)S(1)} %get-tuple-element.61), channel_id=1, source_target_pairs={{1,0},{2,1},{3,2},{5,4},{6,5},{7,6},{9,8},{10,9},{11,10},{13,12},{... | collective-permute-start | bytes 24584 | tf_op jit(solution)/shard_map/ppermute | solution.py:33
  61.4 5.9 %collective-permute-start.11 = (f32[2,1,1,1024]{3,2,1,0:T(1,128)S(1)}, f32[2,1,1,1024]{3,2,1,0:T(1,128)S(1)}, u32[]{:S(2)}, u32[]{:S(2)}) collective-permute-start(f32[2,1,1,1024]{3,2,1,0:T(1,128)S(1)} %get-tuple-element.59), channel_id=1, source_target_pairs={{1,0},{2,1},{3,2},{5,4},{6,5},{7,6},{9,8},{10,9},{11,10},{13,12},{... | collective-permute-start | bytes 24584 | tf_op jit(solution)/shard_map/ppermute | solution.py:33
  62.7 5.9 %collective-permute-start.12 = (f32[2,1,1,1024]{3,2,1,0:T(1,128)S(1)}, f32[2,1,1,1024]{3,2,1,0:T(1,128)S(1)}, u32[]{:S(2)}, u32[]{:S(2)}) collective-permute-start(f32[2,1,1,1024]{3,2,1,0:T(1,128)S(1)} %get-tuple-element.58), channel_id=1, source_target_pairs={{0,1},{1,2},{2,3},{4,5},{5,6},{6,7},{8,9},{9,10},{10,11},{12,13},{... | collective-permute-start | bytes 24584 | tf_op jit(solution)/shard_map/ppermute | solution.py:30
  69.9 6.1 %collective-permute-start.13 = (f32[2,1,1,1024]{3,2,1,0:T(1,128)S(1)}, f32[2,1,1,1024]{3,2,1,0:T(1,128)S(1)}, u32[]{:S(2)}, u32[]{:S(2)}) collective-permute-start(f32[2,1,1,1024]{3,2,1,0:T(1,128)S(1)} %get-tuple-element.57), channel_id=1, source_target_pairs={{1,0},{2,1},{3,2},{5,4},{6,5},{7,6},{9,8},{10,9},{11,10},{13,12},{... | collective-permute-start | bytes 24584 | tf_op jit(solution)/shard_map/ppermute | solution.py:33
  71.2 6.2 %collective-permute-start.14 = (f32[2,1,1,1024]{3,2,1,0:T(1,128)S(1)}, f32[2,1,1,1024]{3,2,1,0:T(1,128)S(1)}, u32[]{:S(2)}, u32[]{:S(2)}) collective-permute-start(f32[2,1,1,1024]{3,2,1,0:T(1,128)S(1)} %get-tuple-element.56), channel_id=1, source_target_pairs={{0,1},{1,2},{2,3},{4,5},{5,6},{6,7},{8,9},{9,10},{10,11},{12,13},{... | collective-permute-start | bytes 24584 | tf_op jit(solution)/shard_map/ppermute | solution.py:30
  78.6 6.1 %collective-permute-start.15 = (f32[2,1,1,1024]{3,2,1,0:T(1,128)S(1)}, f32[2,1,1,1024]{3,2,1,0:T(1,128)S(1)}, u32[]{:S(2)}, u32[]{:S(2)}) collective-permute-start(f32[2,1,1,1024]{3,2,1,0:T(1,128)S(1)} %get-tuple-element.55), channel_id=1, source_target_pairs={{1,0},{2,1},{3,2},{5,4},{6,5},{7,6},{9,8},{10,9},{11,10},{13,12},{... | collective-permute-start | bytes 24584 | tf_op jit(solution)/shard_map/ppermute | solution.py:33
  79.9 6.2 %collective-permute-start.16 = (f32[2,1,1,1024]{3,2,1,0:T(1,128)S(1)}, f32[2,1,1,1024]{3,2,1,0:T(1,128)S(1)}, u32[]{:S(2)}, u32[]{:S(2)}) collective-permute-start(f32[2,1,1,1024]{3,2,1,0:T(1,128)S(1)} %get-tuple-element.54), channel_id=1, source_target_pairs={{0,1},{1,2},{2,3},{4,5},{5,6},{6,7},{8,9},{9,10},{10,11},{12,13},{... | collective-permute-start | bytes 24584 | tf_op jit(solution)/shard_map/ppermute | solution.py:30
  87.5 6.3 %collective-permute-start.17 = (f32[2,1,1,1024]{3,2,1,0:T(1,128)S(1)}, f32[2,1,1,1024]{3,2,1,0:T(1,128)S(1)}, u32[]{:S(2)}, u32[]{:S(2)}) collective-permute-start(f32[2,1,1,1024]{3,2,1,0:T(1,128)S(1)} %get-tuple-element.53), channel_id=1, source_target_pairs={{1,0},{2,1},{3,2},{5,4},{6,5},{7,6},{9,8},{10,9},{11,10},{13,12},{... | collective-permute-start | bytes 24584 | tf_op jit(solution)/shard_map/ppermute | solution.py:33
  88.8 6.2 %collective-permute-start.18 = (f32[2,1,1,1024]{3,2,1,0:T(1,128)S(1)}, f32[2,1,1,1024]{3,2,1,0:T(1,128)S(1)}, u32[]{:S(2)}, u32[]{:S(2)}) collective-permute-start(f32[2,1,1,1024]{3,2,1,0:T(1,128)S(1)} %get-tuple-element.52), channel_id=1, source_target_pairs={{0,1},{1,2},{2,3},{4,5},{5,6},{6,7},{8,9},{9,10},{10,11},{12,13},{... | collective-permute-start | bytes 24584 | tf_op jit(solution)/shard_map/ppermute | solution.py:30
  96.6 2.0 %collective-permute-start.19 = (f32[2,1,64,1024]{3,2,1,0:T(8,128)S(1)}, f32[2,1,64,1024]{3,2,1,0:T(8,128)S(1)}, u32[]{:S(2)}, u32[]{:S(2)}) collective-permute-start(f32[2,1,64,1024]{3,2,1,0:T(8,128)S(1)} %pad_maximum_fusion.17), channel_id=1, source_target_pairs={{0,4},{4,0},{8,12},{12,8},{16,20},{20,16},{24,28},{28,24},{1,5},{5... | collective-permute-start | bytes 1572872 | tf_op jit(solution)/shard_map/ppermute | solution.py:22
  98.8 14.0 %collective-permute-start.20 = (f32[2,1,64,1024]{3,2,1,0:T(8,128)S(1)}, f32[2,1,64,1024]{3,2,1,0:T(8,128)S(1)}, u32[]{:S(2)}, u32[]{:S(2)}) collective-permute-start(f32[2,1,64,1024]{3,2,1,0:T(8,128)S(1)} %fusion.58), channel_id=1, source_target_pairs={{0,8},{4,12},{8,0},{12,4},{16,24},{20,28},{24,16},{28,20},{1,9},{5... | collective-permute-start | bytes 1572872 | tf_op jit(solution)/shard_map/ppermute | solution.py:22
  113.4 7.6 %collective-permute-start.21 = (f32[1,64,1024]{2,1,0:T(8,128)S(1)}, f32[1,64,1024]{2,1,0:T(8,128)S(1)}, u32[]{:S(2)}, u32[]{:S(2)}) collective-permute-start(f32[1,64,1024]{2,1,0:T(8,128)S(1)} %fusion.74), channel_id=1, source_target_pairs={{0,16},{4,20},{8,24},{12,28},{16,0},{20,4},{24,8},{28,12},{1,17},{... | collective-permute-start | bytes 786440 | tf_op jit(solution)/shard_map/ppermute | solution.py:22
where the time goes:
time: 122 us
  starting transfers between devices  55.8 us (46%)
  waiting for transfers between devices  50.7 us (42%)
  other arithmetic  12.8 us (10%)
  between operations  1.62 us (1%)
    ppermute x8, starting transfers between devices, padded_2(): lax.ppermute(lax.slice_in_dim(block, block.shape[dim] - width, None, axis...  37.5 us
    ppermute x6, waiting for transfers between devices, from_partner(): return lax.ppermute(value, axis, pairs)  37.5 us
    ppermute x8, starting transfers between devices, padded_2(): lax.ppermute(lax.slice_in_dim(block, 0, width, axis=dim), axis, backward)  10.3 us
    ppermute x8, waiting for transfers between devices, padded_2(): lax.ppermute(lax.slice_in_dim(block, block.shape[dim] - width, None, axis...  9.03 us
    ppermute x6, starting transfers between devices, from_partner(): return lax.ppermute(value, axis, pairs)  7.9 us
    ppermute x8, waiting for transfers between devices, padded_2(): lax.ppermute(lax.slice_in_dim(block, 0, width, axis=dim), axis, backward)  4.22 us
    sub x7, other arithmetic, spatial(): diagonal * centre - coupled - courant_rows * below - courant_cols * before  2.98 us
  transfers between devices with their start and end apart: 22, of which 13 were waited for; matrix products, arithmetic and copies ran while one was open for 0% of the time, Pallas kernels for 0%

commit v1 on v0

--- a/solution.py
+++ b/solution.py
@@ -1,8 +1,11 @@
+import functools
 import math
 
 import jax
 import jax.numpy as jnp
 from jax import lax
+from jax.experimental import pallas as pl
+from jax.experimental.pallas import tpu as pltpu
 from jax.sharding import PartitionSpec as P
 
 SWEEPS = 2
@@ -207,8 +210,415 @@
     return signal * jnp.exp(-log_alpha * step_float / total_steps)[:, None, None]
 
 
+LANES = 128
+HALO = 8
+SIDES = [(0, -1), (0, 1), (-1, 0), (-1, -1), (-1, 1), (1, 0), (1, -1), (1, 1)]
+
+
+def patch_place(index):
+    chip = index // 2
+    return 2 * (chip + chip // 2 * (5 - 2 * chip)) + index % 2
+
+
+def sublane_constants():
+    field = lax.broadcasted_iota(jnp.int32, (8, LANES), 0)
+    decay = circulant_alpha ** (1.0 / 8)
+    real = jnp.full((8, LANES), 1.0 - decay, jnp.float32)
+    turn = jnp.zeros((8, LANES), jnp.float32)
+    real = jnp.where(field == 4, 1.0 + decay, real)
+    for k in (1, 2, 3):
+        theta = 2.0 * math.pi * k / 8
+        both = field % 4 == k
+        real = jnp.where(both, 1.0 - decay * math.cos(theta), real)
+        sine = decay * math.sin(theta)
+        turn = jnp.where(field == k, sine, jnp.where(field == k + 4, -sine, turn))
+    return real, turn
+
+
+def forward_eight(x):
+    root = math.sqrt(0.5)
+    s = [x[t] + x[t + 4] for t in range(4)]
+    d = [x[t] - x[t + 4] for t in range(4)]
+    even, odd = s[0] + s[2], s[1] + s[3]
+    less, more = root * (d[1] - d[3]), root * (d[1] + d[3])
+    return [
+        even + odd, d[0] + less, s[0] - s[2], d[0] - less,
+        even - odd, -d[2] - more, s[3] - s[1], d[2] - more,
+    ]
+
+
+def backward_eight(f):
+    root = math.sqrt(0.5)
+    x0, r1, r2, r3, x4, i1, i2, i3 = f
+    plus, minus = x0 + x4, x0 - x4
+    even = [plus + 2.0 * r2, minus - 2.0 * i2, plus - 2.0 * r2, minus + 2.0 * i2]
+    less, total = r1 - r3, i1 + i3
+    odd = [
+        2.0 * (r1 + r3), 2.0 * root * (less - total),
+        2.0 * (i3 - i1), -2.0 * root * (less + total),
+    ]
+    return [even[t] + odd[t] for t in range(4)] + [even[t] - odd[t] for t in range(4)]
+
+
+def patch_kernel(
+    rows, row_count, rhs, kappa, out,
+    arrived, leaving, kap, b_m, b_s, v_a, v_b, u_a,
+    coef, inv_r, inv_t, packed, from_left, from_right,
+    go_s, go_r, back_s, back_r, halo_s, halo_r, kap_s, kap_r, local,
+):
+    mesh_id = pl.DeviceIdType.MESH
+    me, z = lax.axis_index("tm"), lax.axis_index("row")
+    p = patch_place(me)
+    ext = rows + 2 * HALO
+    groups = rows // 8
+
+    def there(dp, dz):
+        ok = None
+        for delta, at, count in ((dp, p, 8), (dz, z, row_count)):
+            if delta:
+                good = at > 0 if delta < 0 else at < count - 1
+                ok = good if ok is None else jnp.logical_and(ok, good)
+        return ok
+
+    def neighbour(dp, dz):
+        return (patch_place((p + dp + 8) % 8), z + dz)
+
+    barrier = pltpu.get_barrier_semaphore()
+    for d in range(1, 8):
+        pl.semaphore_signal(barrier, inc=1, device_id=((me + d) % 8, z), device_id_type=mesh_id)
+    expected = jnp.int32(7)
+    for dp, dz in SIDES:
+        if dz == 0:
+            continue
+        ok = there(dp, dz)
+        expected = expected + ok.astype(jnp.int32)
+
+        @pl.when(ok)
+        def _():
+            pl.semaphore_signal(
+                barrier, inc=1, device_id=neighbour(dp, dz), device_id_type=mesh_id
+            )
+
+    own_rhs = pltpu.make_async_copy(
+        rhs.at[:, pl.ds(pl.multiple_of(p * LANES, LANES), LANES)], arrived.at[me], local.at[0]
+    )
+    own_kap = pltpu.make_async_copy(kappa, kap.at[pl.ds(HALO, rows)], local.at[1])
+    own_rhs.start()
+    own_kap.start()
+    pl.semaphore_wait(barrier, expected)
+
+    def go_copy(d):
+        peer = (me + d) % 8
+        columns = pl.ds(pl.multiple_of(patch_place(peer) * LANES, LANES), LANES)
+        return pltpu.make_async_remote_copy(
+            src_ref=rhs.at[:, columns], dst_ref=arrived.at[me],
+            send_sem=go_s.at[d], recv_sem=go_r.at[d],
+            device_id=(peer, z), device_id_type=mesh_id,
+        )
+
+    def go_arrival(d):
+        peer = (me + 8 - d) % 8
+        return pltpu.make_async_remote_copy(
+            src_ref=rhs.at[:, pl.ds(0, LANES)], dst_ref=arrived.at[peer],
+            send_sem=go_s.at[d], recv_sem=go_r.at[d],
+            device_id=(peer, z), device_id_type=mesh_id,
+        )
+
+    def kap_copy(dz):
+        first, last = (0, HALO + rows) if dz < 0 else (rows - HALO, 0)
+        which = (dz + 1) // 2
+        return pltpu.make_async_remote_copy(
+            src_ref=kappa.at[pl.ds(first, HALO)], dst_ref=kap.at[pl.ds(last, HALO)],
+            send_sem=kap_s.at[which], recv_sem=kap_r.at[which],
+            device_id=(me, z + dz), device_id_type=mesh_id,
+        )
+
+    for dz in (-1, 1):
+        @pl.when(there(0, dz))
+        def _():
+            kap_copy(dz).start()
+
+    for d in range(1, 8):
+        go_copy(d).start()
+
+    own_kap.wait()
+    for dz in (-1, 1):
+        lost = HALO + rows if dz < 0 else 0
+
+        @pl.when(there(0, -dz))
+        def _():
+            kap_copy(dz).wait_recv()
+
+        @pl.when(jnp.logical_not(there(0, -dz)))
+        def _():
+            kap[pl.ds(lost, HALO), :] = jnp.zeros((HALO, kap.shape[1]), jnp.float32)
+
+    lane = lax.broadcasted_iota(jnp.int32, (8, LANES), 1)
+    lane_all = lax.broadcasted_iota(jnp.int32, (ext, LANES), 1)
+
+    def kap_block(which):
+        return kap[:, pl.ds(pl.multiple_of(which * LANES, LANES), LANES)]
+
+    right_in = (p < 7).astype(jnp.float32)
+    left_in = (p > 0).astype(jnp.float32)
+    side_in = jnp.where(lane_all < 64, right_in, left_in)
+    row_at = lax.broadcasted_iota(jnp.int32, (ext, LANES), 0)
+    top_in = (z > 0).astype(jnp.float32)
+    low_in = (z < row_count - 1).astype(jnp.float32)
+    row_in = jnp.where(row_at < HALO, top_in, jnp.where(row_at >= HALO + rows, low_in, 1.0))
+    k_m = kap_block(p)
+    k_s = jnp.where(lane_all < 64, kap_block((p + 1) % 8), kap_block((p + 7) % 8)) * side_in
+    turned = [pltpu.roll(k, 1, 1) for k in (k_m, k_s)]
+    turned_up = [pltpu.roll(k, LANES - 1, 1) for k in (k_m, k_s)]
+    for side, k in enumerate((k_m, k_s)):
+        north = 0.5 * (k + pltpu.roll(k, ext - 1, 0))
+        south = 0.5 * (k + pltpu.roll(k, 1, 0))
+        east = 0.5 * (k + jnp.where(lane_all == LANES - 1, turned_up[1 - side], turned_up[side]))
+        west = 0.5 * (k + jnp.where(lane_all == 0, turned[1 - side], turned[side]))
+        diagonal = north + south + east + west + (courant_rows + courant_cols)
+        inside = row_in if side == 0 else row_in * side_in
+        parts = (north, south + courant_rows, east, west + courant_cols, diagonal, inside)
+        for number, part in enumerate(parts):
+            u_a[pl.ds((side * 6 + number) * ext, ext), :] = part
+
+    shift_real, shift_turn = sublane_constants()
+    shift_square = shift_turn * shift_turn
+
+    def spread(g, carry):
+        for side in range(2):
+            tiles = [
+                u_a[pl.ds(pl.multiple_of((side * 6 + number) * ext + 8 * g, 8), 8), :]
+                for number in range(6)
+            ]
+            for i in range(8):
+                at = pl.ds(pl.multiple_of(64 * g + 8 * i, 8), 8)
+                wide = [jnp.broadcast_to(tile[i : i + 1, :], (8, LANES)) for tile in tiles]
+                for number in range(4):
+                    coef[side * 4 + number, at, :] = wide[number]
+                diag_real = wide[4] + shift_real
+                scale = wide[5] / (diag_real * diag_real + shift_square)
+                inv_r[side, at, :] = diag_real * scale
+                inv_t[side, at, :] = shift_turn * scale
+        return carry
+
+    lax.fori_loop(0, ext // 8, spread, 0)
+
+    own_rhs.wait()
+    for d in range(1, 8):
+        go_arrival(d).wait_recv()
+
+    log_alpha = math.log(circulant_alpha)
+
+    def transform(g, carry):
+        tile = pl.ds(pl.multiple_of(8 * g, 8), 8)
+        steps = [arrived[t, tile, :] * math.exp(log_alpha * t / 8) for t in range(8)]
+        for f, value in enumerate(forward_eight(steps)):
+            b_m[pl.ds(64 * (g + 1) + f, 8, stride=8), :] = value
+        edges = jnp.zeros((8, LANES), jnp.float32)
+        for i in range(8):
+            line = b_m[pl.ds(pl.multiple_of(64 * (g + 1) + 8 * i, 8), 8), :]
+            edges = jnp.where(lane // 16 == i, pltpu.roll(line, 8 + 16 * i, 1), edges)
+        packed[tile, :] = edges
+        return carry
+
+    lax.fori_loop(0, groups, transform, 0)
+
+    def halo_copy(number):
+        dp, dz = SIDES[number]
+        if dp == 0:
+            first = HALO if dz < 0 else rows
+            source = b_m.at[pl.ds(8 * first, 8 * HALO)]
+        else:
+            first, count = {0: (0, groups), -1: (0, 1), 1: (groups - 1, 1)}[dz]
+            source = packed.at[pl.ds(8 * first, 8 * count)]
+        copy = pltpu.make_async_remote_copy(
+            src_ref=source, dst_ref=halo_target(number),
+            send_sem=halo_s.at[number], recv_sem=halo_r.at[number],
+            device_id=neighbour(dp, dz), device_id_type=mesh_id,
+        )
+        return copy
+
+    def halo_target(number):
+        dp, dz = SIDES[number]
+        if dp == 0:
+            return b_m.at[pl.ds(8 * (HALO + rows if dz < 0 else 0), 8 * HALO)]
+        last, count = {0: (1, groups), -1: (groups + 1, 1), 1: (0, 1)}[dz]
+        return (from_right if dp < 0 else from_left).at[pl.ds(8 * last, 8 * count)]
+
+    for number, (dp, dz) in enumerate(SIDES):
+        @pl.when(there(dp, dz))
+        def _():
+            halo_copy(number).start()
+
+    for number, (dp, dz) in enumerate(SIDES):
+        @pl.when(there(-dp, -dz))
+        def _():
+            halo_copy(number).wait_recv()
+
+        @pl.when(jnp.logical_not(there(-dp, -dz)))
+        def _():
+            target = halo_target(number)
+            target[...] = jnp.zeros(target.shape, jnp.float32)
+
+    weights = step_weights(DEGREE) * SWEEPS
+    edge = jnp.zeros((8, LANES), jnp.float32)
+    for ref in (v_a, v_b):
+        for side in range(2):
+            ref[side, pl.ds(0, 8), :] = edge
+            ref[side, pl.ds(8 * (ext + 1), 8), :] = edge
+
+    def begin(g, carry):
+        tile = pl.ds(pl.multiple_of(8 * g, 8), 8)
+        both = jnp.where(lane % 16 < 8, from_left[tile, :], from_right[tile, :])
+        for i in range(8):
+            at = pl.ds(pl.multiple_of(64 * g + 8 * i, 8), 8)
+            after = pl.ds(pl.multiple_of(64 * g + 8 * i + 8, 8), 8)
+            line = pltpu.roll(both, 120 - 16 * i, 1)
+            b_s[at, :] = line
+            for side, value in enumerate((b_m[at, :], line)):
+                v_a[side, after, :] = weights[0] * (
+                    inv_r[side, at, :] * value + inv_t[side, at, :] * pltpu.roll(value, 4, 0)
+                )
+        return carry
+
+    lax.fori_loop(0, ext // 8, begin, 0)
+
+    def step(old, new, weight, last):
+        def body(g, carry):
+            for i in range(8):
+                at = pl.ds(pl.multiple_of(64 * g + 8 * i, 8), 8)
+                mid = pl.ds(pl.multiple_of(64 * g + 8 * i + 8, 8), 8)
+                above = pl.ds(pl.multiple_of(64 * g + 8 * i + 16, 8), 8)
+                here = [old[side, mid, :] for side in range(2)]
+                ups = [pltpu.roll(x, LANES - 1, 1) for x in here]
+                downs = [pltpu.roll(x, 1, 1) for x in here]
+                for side in range(1 if last else 2):
+                    total = (b_m if side == 0 else b_s)[at, :]
+                    total = total + coef[4 * side, at, :] * old[side, above, :]
+                    total = total + coef[4 * side + 1, at, :] * old[side, at, :]
+                    total = total + coef[4 * side + 2, at, :] * jnp.where(
+                        lane == LANES - 1, ups[1 - side], ups[side]
+                    )
+                    total = total + coef[4 * side + 3, at, :] * jnp.where(
+                        lane == 0, downs[1 - side], downs[side]
+                    )
+                    change = inv_r[side, at, :] * total + inv_t[side, at, :] * pltpu.roll(
+                        total, 4, 0
+                    )
+                    new[side, mid, :] = (1.0 - weight) * here[side] + weight * change
+            return carry
+
+        if last:
+            lax.fori_loop(1, groups + 1, body, 0)
+        else:
+            lax.fori_loop(0, ext // 8, body, 0)
+
+    old, new = v_a, v_b
+    for number in range(1, len(weights)):
+        step(old, new, weights[number], number == len(weights) - 1)
+        old, new = new, old
+
+    def inverse(g, carry):
+        tile = pl.ds(pl.multiple_of(8 * g, 8), 8)
+        fields = [old[0, pl.ds(64 * (g + 1) + 8 + f, 8, stride=8), :] for f in range(8)]
+        for t, value in enumerate(backward_eight(fields)):
+            leaving[t, tile, :] = value * (math.exp(-log_alpha * t / 8) / 8)
+        return carry
+
+    lax.fori_loop(0, groups, inverse, 0)
+
+    columns = pl.ds(pl.multiple_of(p * LANES, LANES), LANES)
+
+    def back_copy(d):
+        peer = (me + d) % 8
+        return pltpu.make_async_remote_copy(
+            src_ref=leaving.at[peer], dst_ref=out.at[:, columns],
+            send_sem=back_s.at[d], recv_sem=back_r.at[d],
+            device_id=(peer, z), device_id_type=mesh_id,
+        )
+
+    def back_arrival(d):
+        peer = (me + 8 - d) % 8
+        theirs = pl.ds(pl.multiple_of(patch_place(peer) * LANES, LANES), LANES)
+        return pltpu.make_async_remote_copy(
+            src_ref=leaving.at[peer], dst_ref=out.at[:, theirs],
+            send_sem=back_s.at[d], recv_sem=back_r.at[d],
+            device_id=(peer, z), device_id_type=mesh_id,
+        )
+
+    for d in range(1, 8):
+        back_copy(d).start()
+    own_out = pltpu.make_async_copy(leaving.at[me], out.at[:, columns], local.at[2])
+    own_out.start()
+
+    for dz in (-1, 1):
+        @pl.when(there(0, dz))
+        def _():
+            kap_copy(dz).wait_send()
+
+    for d in range(1, 8):
+        go_copy(d).wait_send()
+    for number, (dp, dz) in enumerate(SIDES):
+        @pl.when(there(dp, dz))
+        def _():
+            halo_copy(number).wait_send()
+
+    own_out.wait()
+    for d in range(1, 8):
+        back_arrival(d).wait_recv()
+    for d in range(1, 8):
+        back_copy(d).wait_send()
+
+
+def patch_body(row_count, right_side, kappa):
+    rows, width = kappa.shape
+    ext = rows + 2 * HALO
+    f32 = jnp.float32
+    dma = pltpu.SemaphoreType.DMA
+    result = pl.pallas_call(
+        functools.partial(patch_kernel, rows, row_count),
+        out_shape=jax.ShapeDtypeStruct((rows, width), f32),
+        in_specs=[pl.BlockSpec(memory_space=pl.ANY)] * 2,
+        out_specs=pl.BlockSpec(memory_space=pltpu.VMEM),
+        scratch_shapes=[
+            pltpu.VMEM((8, rows, LANES), f32),
+            pltpu.VMEM((8, rows, LANES), f32),
+            pltpu.VMEM((ext, width), f32),
+            pltpu.VMEM((8 * ext, LANES), f32),
+            pltpu.VMEM((8 * ext, LANES), f32),
+            pltpu.VMEM((2, 8 * (ext + 2), LANES), f32),
+            pltpu.VMEM((2, 8 * (ext + 2), LANES), f32),
+            pltpu.VMEM((12 * ext, LANES), f32),
+            pltpu.VMEM((8, 8 * ext, LANES), f32),
+            pltpu.VMEM((2, 8 * ext, LANES), f32),
+            pltpu.VMEM((2, 8 * ext, LANES), f32),
+            pltpu.VMEM((rows, LANES), f32),
+            pltpu.VMEM((ext, LANES), f32),
+            pltpu.VMEM((ext, LANES), f32),
+            dma((8,)), dma((8,)), dma((8,)), dma((8,)), dma((8,)), dma((8,)),
+            dma((2,)), dma((2,)), dma((3,)),
+        ],
+        compiler_params=pltpu.CompilerParams(
+            collective_id=0, has_side_effects=True, vmem_limit_bytes=24 * 2**20
+        ),
+        name="patch_solve",
+    )(right_side.reshape(rows, width), kappa)
+    return result.reshape(right_side.shape)
+
+
 def solution(mesh):
     placed = (P("tm", "row", None), P("row", None))
+    tm_size, row_count = mesh.shape["tm"], mesh.shape["row"]
+
+    def local(right_side, kappa):
+        fits = (
+            tm_size == 8 and right_side.shape[0] == 1
+            and kappa.shape[1] == tm_size * LANES and kappa.shape[0] % 8 == 0
+        )
+        if fits:
+            return patch_body(row_count, right_side, kappa)
+        return body(right_side, kappa)
+
     return jax.shard_map(
-        body, mesh=mesh, in_specs=placed, out_specs=P("tm", "row", None), check_vma=False
+        local, mesh=mesh, in_specs=placed, out_specs=P("tm", "row", None), check_vma=False
     )

time: 122 us -> 29.4 us (0.24)
  starting transfers between devices: 55.8 us -> 0 us
  waiting for transfers between devices: 50.7 us -> 0 us
  Pallas kernels: 0 us -> 26.6 us
  other arithmetic: 12.8 us -> 0 us
  local copies, waits for them, and re-layouts: 0.87 us -> 2.6 us
  between operations: 1.62 us -> 0.01 us
    ppermute x22 -> x0, starting transfers between devices: 55.8 us -> none  [the longest x8 37.5 us: padded_2(): lax.ppermute(lax.slice_in_dim(block, block.shape[dim] - width, None, axis...]
    ppermute x22 -> x0, waiting for transfers between devices: 50.7 us -> none  [the longest x6 37.5 us: from_partner(): return lax.ppermute(value, axis, pairs)]
    pallas_call x0 -> x1, Pallas kernels: none -> 26.6 us  [patch_body(): pl.pallas_call(functools.partial(patch_kernel, rows, row_count), out_shap...]
    sub x21 -> x0, other arithmetic: 3.93 us -> none  [the longest x7 2.98 us: spatial(): diagonal * centre - coupled - courant_rows * below - courant_cols * before]
    add x15 -> x0, other arithmetic: 2.74 us -> none  [the longest x7 1.94 us: solve_each(): state = state + weight * jnp.stack([corr_real, corr_imag])]
    concatenate x8 -> x0, other arithmetic: 2.09 us -> none  [padded_2(): block = jnp.concatenate([low, block, high], axis=dim)]
    mul x3 -> x0, other arithmetic: 1.87 us -> none  [the longest x1 1.03 us: body(): right_side * jnp.exp(log_alpha * step_float / total_steps)[:, None, None]]
    unnamed x4 -> x5, local copies, waits for them, and re-layouts: 0.76 us -> 2.6 us
  transfers between devices with their start and end apart: 22 -> 0, of which waited for: 13 -> 0; matrix products, arithmetic and copies ran while one was open for 0% -> 0% of each run, Pallas kernels for 0% -> 0%
where the time goes in v1:
time: 29.4 us; the launch traced here: 29.2 us
  Pallas kernels  26.6 us (90%)
  local copies, waits for them, and re-layouts  2.6 us (9%)
    pallas_call x1, Pallas kernels, patch_body(): pl.pallas_call(functools.partial(patch_kernel, rows, row_count), out_shap...  26.6 us
    unnamed x5, local copies, waits for them, and re-layouts  2.6 us

profile of v1, /device:TPU:0, one launch (start us, length us, event | category | flops | bytes accessed | tf_op | source)
XLA Modules:
  0.0 29.2 jit_solution(18254820873233386699)
XLA Ops:
  0.0 0.0 copy-start
  0.0 0.9 %copy-done = f32[1,64,1024]{2,1,0:T(8,128)S(1)} copy-done((f32[1,64,1024]{2,1,0:T(8,128)S(1)}, f32[1,64,1024]{2,1,0:T(8,128)}, u32[]{:S(2)}) %copy-start) | copy-done | bytes 262168
  1.0 0.0 copy-start.1
  1.0 0.9 %copy-done.1 = f32[64,1024]{1,0:T(8,128)S(1)} copy-done((f32[64,1024]{1,0:T(8,128)S(1)}, f32[64,1024]{1,0:T(8,128)}, u32[]{:S(2)}) %copy-start.1) | copy-done | bytes 262168
  1.9 26.6 %patch_solve.1 = f32[64,1024]{1,0:T(8,128)S(1)} custom-call(f32[64,1024]{1,0:T(8,128)S(1)} %bitcast.3, f32[64,1024]{1,0:T(8,128)S(1)} %copy-done.1), custom_call_target="tpu_custom_call" | custom-call | tf_op jit(solution)/shard_map/patch_solve/pallas_call | solution.py:578
  28.5 0.7 %copy.4 = f32[1,64,1024]{2,1,0:T(8,128)} copy(f32[1,64,1024]{2,1,0:T(8,128)S(1)} %bitcast.2) | data formatting | bytes 524288
Async XLA Ops:
  0.0 0.9 %copy-start = (f32[1,64,1024]{2,1,0:T(8,128)S(1)}, f32[1,64,1024]{2,1,0:T(8,128)}, u32[]{:S(2)}) copy-start(f32[1,64,1024]{2,1,0:T(8,128)} %param.2) | copy-start | bytes 786436
  1.0 0.9 %copy-start.1 = (f32[64,1024]{1,0:T(8,128)S(1)}, f32[64,1024]{1,0:T(8,128)}, u32[]{:S(2)}) copy-start(f32[64,1024]{1,0:T(8,128)} %kappa.1) | copy-start | bytes 786436

commit v2 on v1

--- a/solution.py
+++ b/solution.py
@@ -221,18 +221,17 @@
 
 
 def sublane_constants():
-    field = lax.broadcasted_iota(jnp.int32, (8, LANES), 0)
+    field = lax.broadcasted_iota(jnp.int32, (8, LANES), 0) % 4
     decay = circulant_alpha ** (1.0 / 8)
-    real = jnp.full((8, LANES), 1.0 - decay, jnp.float32)
+    real = jnp.zeros((8, LANES), jnp.float32)
     turn = jnp.zeros((8, LANES), jnp.float32)
-    real = jnp.where(field == 4, 1.0 + decay, real)
     for k in (1, 2, 3):
         theta = 2.0 * math.pi * k / 8
-        both = field % 4 == k
-        real = jnp.where(both, 1.0 - decay * math.cos(theta), real)
-        sine = decay * math.sin(theta)
-        turn = jnp.where(field == k, sine, jnp.where(field == k + 4, -sine, turn))
-    return real, turn
+        real = jnp.where(field == k, 1.0 - decay * math.cos(theta), real)
+        turn = jnp.where(field == k, decay * math.sin(theta), turn)
+    real_a = jnp.where(field == 0, 1.0 - decay, real)
+    real_b = jnp.where(field == 0, 1.0 + decay, real)
+    return real_a, real_b, turn
 
 
 def forward_eight(x):
@@ -262,8 +261,8 @@
 
 def patch_kernel(
     rows, row_count, rhs, kappa, out,
-    arrived, leaving, kap, b_m, b_s, v_a, v_b, u_a,
-    coef, inv_r, inv_t, packed, from_left, from_right,
+    arrived, leaving, kap, rhs_f, v_a, v_b, u_a,
+    coef, inv, packed, from_left, from_right, row_out, row_in_f,
     go_s, go_r, back_s, back_r, halo_s, halo_r, kap_s, kap_r, local,
 ):
     mesh_id = pl.DeviceIdType.MESH
@@ -271,6 +270,7 @@
     p = patch_place(me)
     ext = rows + 2 * HALO
     groups = rows // 8
+    pairs = ext // 2
 
     def there(dp, dz):
         ok = None
@@ -381,27 +381,40 @@
         for number, part in enumerate(parts):
             u_a[pl.ds((side * 6 + number) * ext, ext), :] = part
 
-    shift_real, shift_turn = sublane_constants()
+    shift_a, shift_b, shift_turn = sublane_constants()
     shift_square = shift_turn * shift_turn
+    upper = lax.broadcasted_iota(jnp.int32, (8, LANES), 0) < 4
 
     def spread(g, carry):
         for side in range(2):
-            tiles = [
-                u_a[pl.ds(pl.multiple_of((side * 6 + number) * ext + 8 * g, 8), 8), :]
+            both = [
+                [
+                    u_a[pl.ds(pl.multiple_of((side * 6 + number) * ext + half + 8 * g, 8), 8), :]
+                    for half in (0, pairs)
+                ]
                 for number in range(6)
             ]
             for i in range(8):
                 at = pl.ds(pl.multiple_of(64 * g + 8 * i, 8), 8)
-                wide = [jnp.broadcast_to(tile[i : i + 1, :], (8, LANES)) for tile in tiles]
+                wide = [
+                    jnp.where(
+                        upper,
+                        jnp.broadcast_to(first[i : i + 1, :], (8, LANES)),
+                        jnp.broadcast_to(second[i : i + 1, :], (8, LANES)),
+                    )
+                    for first, second in both
+                ]
                 for number in range(4):
                     coef[side * 4 + number, at, :] = wide[number]
-                diag_real = wide[4] + shift_real
-                scale = wide[5] / (diag_real * diag_real + shift_square)
-                inv_r[side, at, :] = diag_real * scale
-                inv_t[side, at, :] = shift_turn * scale
+                diag_a, diag_b = wide[4] + shift_a, wide[4] + shift_b
+                scale_a = wide[5] / (diag_a * diag_a + shift_square)
+                scale_b = wide[5] / (diag_b * diag_b + shift_square)
+                inv[side * 3, at, :] = diag_a * scale_a
+                inv[side * 3 + 1, at, :] = diag_b * scale_b
+                inv[side * 3 + 2, at, :] = shift_turn * scale_a
         return carry
 
-    lax.fori_loop(0, ext // 8, spread, 0)
+    lax.fori_loop(0, pairs // 8, spread, 0)
 
     own_rhs.wait()
     for d in range(1, 8):
@@ -409,25 +422,27 @@
 
     log_alpha = math.log(circulant_alpha)
 
-    def transform(g, carry):
-        tile = pl.ds(pl.multiple_of(8 * g, 8), 8)
+    def strided(row, f, pad):
+        half, pair = row // pairs, row % pairs
+        return pl.ds(8 * (pair + pad) + 4 * half + f % 4, 8, stride=8)
+
+    for g in range(groups):
+        tile = pl.ds(8 * g, 8)
         steps = [arrived[t, tile, :] * math.exp(log_alpha * t / 8) for t in range(8)]
+        edges = jnp.zeros((8, LANES), jnp.float32)
         for f, value in enumerate(forward_eight(steps)):
-            b_m[pl.ds(64 * (g + 1) + f, 8, stride=8), :] = value
-        edges = jnp.zeros((8, LANES), jnp.float32)
-        for i in range(8):
-            line = b_m[pl.ds(pl.multiple_of(64 * (g + 1) + 8 * i, 8), 8), :]
-            edges = jnp.where(lane // 16 == i, pltpu.roll(line, 8 + 16 * i, 1), edges)
+            rhs_f[f // 4, strided(HALO + 8 * g, f, 0), :] = value
+            edges = jnp.where(lane // 16 == f, pltpu.roll(value, 8 + 16 * f, 1), edges)
+            if g == 0:
+                row_out[0, f] = value
+            if g == groups - 1:
+                row_out[1, f] = value
         packed[tile, :] = edges
-        return carry
-
-    lax.fori_loop(0, groups, transform, 0)
 
     def halo_copy(number):
         dp, dz = SIDES[number]
         if dp == 0:
-            first = HALO if dz < 0 else rows
-            source = b_m.at[pl.ds(8 * first, 8 * HALO)]
+            source = row_out.at[0 if dz < 0 else 1]
         else:
             first, count = {0: (0, groups), -1: (0, 1), 1: (groups - 1, 1)}[dz]
             source = packed.at[pl.ds(8 * first, 8 * count)]
@@ -441,7 +456,7 @@
     def halo_target(number):
         dp, dz = SIDES[number]
         if dp == 0:
-            return b_m.at[pl.ds(8 * (HALO + rows if dz < 0 else 0), 8 * HALO)]
+            return row_in_f.at[1 if dz < 0 else 0]
         last, count = {0: (1, groups), -1: (groups + 1, 1), 1: (0, 1)}[dz]
         return (from_right if dp < 0 else from_left).at[pl.ds(8 * last, 8 * count)]
 
@@ -461,71 +476,88 @@
             target[...] = jnp.zeros(target.shape, jnp.float32)
 
     weights = step_weights(DEGREE) * SWEEPS
-    edge = jnp.zeros((8, LANES), jnp.float32)
-    for ref in (v_a, v_b):
-        for side in range(2):
-            ref[side, pl.ds(0, 8), :] = edge
-            ref[side, pl.ds(8 * (ext + 1), 8), :] = edge
+    for g in range(ext // 8):
+        tile = pl.ds(8 * g, 8)
+        both = jnp.where(lane % 16 < 8, from_left[tile, :], from_right[tile, :])
+        for f in range(8):
+            at = strided(8 * g, f, 0)
+            rhs_f[2 + f // 4, at, :] = pltpu.roll(both, 120 - 16 * f, 1)
+            if g == 0:
+                rhs_f[f // 4, at, :] = row_in_f[0, f]
+            if g == ext // 8 - 1:
+                rhs_f[f // 4, at, :] = row_in_f[1, f]
+
+    def close(ref):
+        for which in range(4):
+            ref[which, pl.ds(0, 8), :] = pltpu.roll(ref[which, pl.ds(8 * pairs, 8), :], 4, 0)
+            ref[which, pl.ds(8 * pairs + 8, 8), :] = pltpu.roll(ref[which, pl.ds(8, 8), :], 4, 0)
+
+    chunk = pairs // 2
 
     def begin(g, carry):
-        tile = pl.ds(pl.multiple_of(8 * g, 8), 8)
-        both = jnp.where(lane % 16 < 8, from_left[tile, :], from_right[tile, :])
-        for i in range(8):
-            at = pl.ds(pl.multiple_of(64 * g + 8 * i, 8), 8)
-            after = pl.ds(pl.multiple_of(64 * g + 8 * i + 8, 8), 8)
-            line = pltpu.roll(both, 120 - 16 * i, 1)
-            b_s[at, :] = line
-            for side, value in enumerate((b_m[at, :], line)):
-                v_a[side, after, :] = weights[0] * (
-                    inv_r[side, at, :] * value + inv_t[side, at, :] * pltpu.roll(value, 4, 0)
-                )
+        for i in range(chunk):
+            at = pl.ds(pl.multiple_of(8 * chunk * g + 8 * i, 8), 8)
+            mid = pl.ds(pl.multiple_of(8 * chunk * g + 8 * i + 8, 8), 8)
+            for side in range(2):
+                a, b = rhs_f[2 * side, at, :], rhs_f[2 * side + 1, at, :]
+                turn = inv[3 * side + 2, at, :]
+                v_a[2 * side, mid, :] = weights[0] * (inv[3 * side, at, :] * a + turn * b)
+                v_a[2 * side + 1, mid, :] = weights[0] * (inv[3 * side + 1, at, :] * b - turn * a)
         return carry
 
-    lax.fori_loop(0, ext // 8, begin, 0)
+    lax.fori_loop(0, 2, begin, 0)
+    close(v_a)
 
     def step(old, new, weight, last):
         def body(g, carry):
-            for i in range(8):
-                at = pl.ds(pl.multiple_of(64 * g + 8 * i, 8), 8)
-                mid = pl.ds(pl.multiple_of(64 * g + 8 * i + 8, 8), 8)
-                above = pl.ds(pl.multiple_of(64 * g + 8 * i + 16, 8), 8)
-                here = [old[side, mid, :] for side in range(2)]
+            def tile_of(which, i):
+                return old[which, pl.ds(pl.multiple_of(8 * chunk * g + 8 * i, 8), 8), :]
+
+            before = [tile_of(which, 0) for which in range(4)]
+            here = [tile_of(which, 1) for which in range(4)]
+            for i in range(chunk):
+                at = pl.ds(pl.multiple_of(8 * chunk * g + 8 * i, 8), 8)
+                mid = pl.ds(pl.multiple_of(8 * chunk * g + 8 * i + 8, 8), 8)
+                after = [tile_of(which, i + 2) for which in range(4)]
                 ups = [pltpu.roll(x, LANES - 1, 1) for x in here]
                 downs = [pltpu.roll(x, 1, 1) for x in here]
                 for side in range(1 if last else 2):
-                    total = (b_m if side == 0 else b_s)[at, :]
-                    total = total + coef[4 * side, at, :] * old[side, above, :]
-                    total = total + coef[4 * side + 1, at, :] * old[side, at, :]
-                    total = total + coef[4 * side + 2, at, :] * jnp.where(
-                        lane == LANES - 1, ups[1 - side], ups[side]
+                    north, south, east, west = [coef[4 * side + n, at, :] for n in range(4)]
+                    totals = []
+                    for part in range(2):
+                        own, other = 2 * side + part, 2 * (1 - side) + part
+                        right = jnp.where(lane == LANES - 1, ups[other], ups[own])
+                        left = jnp.where(lane == 0, downs[other], downs[own])
+                        totals.append(
+                            (rhs_f[own, at, :] + north * after[own])
+                            + (south * before[own] + east * right)
+                            + west * left
+                        )
+                    turn = inv[3 * side + 2, at, :]
+                    changes = (
+                        inv[3 * side, at, :] * totals[0] + turn * totals[1],
+                        inv[3 * side + 1, at, :] * totals[1] - turn * totals[0],
                     )
-                    total = total + coef[4 * side + 3, at, :] * jnp.where(
-                        lane == 0, downs[1 - side], downs[side]
-                    )
-                    change = inv_r[side, at, :] * total + inv_t[side, at, :] * pltpu.roll(
-                        total, 4, 0
-                    )
-                    new[side, mid, :] = (1.0 - weight) * here[side] + weight * change
+                    for part in range(2):
+                        own = 2 * side + part
+                        new[own, mid, :] = (1.0 - weight) * here[own] + weight * changes[part]
+                before, here = here, after
             return carry
 
-        if last:
-            lax.fori_loop(1, groups + 1, body, 0)
-        else:
-            lax.fori_loop(0, ext // 8, body, 0)
+        lax.fori_loop(0, 2, body, 0)
+        if not last:
+            close(new)
 
     old, new = v_a, v_b
     for number in range(1, len(weights)):
         step(old, new, weights[number], number == len(weights) - 1)
         old, new = new, old
 
-    def inverse(g, carry):
-        tile = pl.ds(pl.multiple_of(8 * g, 8), 8)
-        fields = [old[0, pl.ds(64 * (g + 1) + 8 + f, 8, stride=8), :] for f in range(8)]
+    for g in range(groups):
+        tile = pl.ds(8 * g, 8)
+        fields = [old[f // 4, strided(HALO + 8 * g, f, 1), :] for f in range(8)]
         for t, value in enumerate(backward_eight(fields)):
             leaving[t, tile, :] = value * (math.exp(-log_alpha * t / 8) / 8)
-        return carry
-
-    lax.fori_loop(0, groups, inverse, 0)
 
     columns = pl.ds(pl.multiple_of(p * LANES, LANES), LANES)
 
@@ -584,22 +616,22 @@
             pltpu.VMEM((8, rows, LANES), f32),
             pltpu.VMEM((8, rows, LANES), f32),
             pltpu.VMEM((ext, width), f32),
-            pltpu.VMEM((8 * ext, LANES), f32),
-            pltpu.VMEM((8 * ext, LANES), f32),
-            pltpu.VMEM((2, 8 * (ext + 2), LANES), f32),
-            pltpu.VMEM((2, 8 * (ext + 2), LANES), f32),
+            pltpu.VMEM((4, 4 * ext, LANES), f32),
+            pltpu.VMEM((4, 4 * (ext + 4), LANES), f32),
+            pltpu.VMEM((4, 4 * (ext + 4), LANES), f32),
             pltpu.VMEM((12 * ext, LANES), f32),
-            pltpu.VMEM((8, 8 * ext, LANES), f32),
-            pltpu.VMEM((2, 8 * ext, LANES), f32),
-            pltpu.VMEM((2, 8 * ext, LANES), f32),
+            pltpu.VMEM((8, 4 * ext, LANES), f32),
+            pltpu.VMEM((6, 4 * ext, LANES), f32),
             pltpu.VMEM((rows, LANES), f32),
             pltpu.VMEM((ext, LANES), f32),
             pltpu.VMEM((ext, LANES), f32),
+            pltpu.VMEM((2, 8, HALO, LANES), f32),
+            pltpu.VMEM((2, 8, HALO, LANES), f32),
             dma((8,)), dma((8,)), dma((8,)), dma((8,)), dma((8,)), dma((8,)),
             dma((2,)), dma((2,)), dma((3,)),
         ],
         compiler_params=pltpu.CompilerParams(
-            collective_id=0, has_side_effects=True, vmem_limit_bytes=24 * 2**20
+            collective_id=0, has_side_effects=True, vmem_limit_bytes=60 * 2**20
         ),
         name="patch_solve",
     )(right_side.reshape(rows, width), kappa)
@@ -613,7 +645,7 @@
     def local(right_side, kappa):
         fits = (
             tm_size == 8 and right_side.shape[0] == 1
-            and kappa.shape[1] == tm_size * LANES and kappa.shape[0] % 8 == 0
+            and kappa.shape[1] == tm_size * LANES and kappa.shape[0] % 16 == 0
         )
         if fits:
             return patch_body(row_count, right_side, kappa)

time: 29.4 us -> 24 us (0.82)
  Pallas kernels: 26.6 us -> 22.2 us
  local copies, waits for them, and re-layouts: 2.6 us -> 1.67 us
    pallas_call x1, Pallas kernels: 26.6 us -> 22.2 us  [patch_body(): pl.pallas_call(functools.partial(patch_kernel, rows, row_count), out_shap...]
    unnamed x5 -> x1, local copies, waits for them, and re-layouts: 2.6 us -> 1.67 us
where the time goes in v2:
time: 24 us; the launch traced here: 23.9 us
  Pallas kernels  22.2 us (92%)
  local copies, waits for them, and re-layouts  1.67 us (7%)
    pallas_call x1, Pallas kernels, patch_body(): pl.pallas_call(functools.partial(patch_kernel, rows, row_count), out_shap...  22.2 us
    unnamed x1, local copies, waits for them, and re-layouts  1.67 us

profile of v2, /device:TPU:0, one launch (start us, length us, event | category | flops | bytes accessed | tf_op | source)
XLA Modules:
  0.0 23.9 jit_solution(15720468959872331158)
XLA Ops:
  0.0 22.2 %patch_solve.1 = f32[64,1024]{1,0:T(8,128)} custom-call(f32[64,1024]{1,0:T(8,128)} %bitcast.3, f32[64,1024]{1,0:T(8,128)} %kappa.1), custom_call_target="tpu_custom_call" | custom-call | tf_op jit(solution)/shard_map/patch_solve/pallas_call | solution.py:610
  22.2 1.7 %copy.4 = f32[1,64,1024]{2,1,0:T(8,128)} copy(f32[1,64,1024]{2,1,0:T(8,128)} %bitcast.2) | data formatting | bytes 524288

commit v3 on v2

--- a/solution.py
+++ b/solution.py
@@ -262,7 +262,7 @@
 def patch_kernel(
     rows, row_count, rhs, kappa, out,
     arrived, leaving, kap, rhs_f, v_a, v_b, u_a,
-    coef, inv, packed, from_left, from_right, row_out, row_in_f,
+    coef, inv, side_f, side_a, side_b, coef_s, inv_s, packed, from_left, from_right, row_out, row_in_f,
     go_s, go_r, back_s, back_r, halo_s, halo_r, kap_s, kap_r, local,
 ):
     mesh_id = pl.DeviceIdType.MESH
@@ -271,6 +271,7 @@
     ext = rows + 2 * HALO
     groups = rows // 8
     pairs = ext // 2
+    packs = pairs // 8
 
     def there(dp, dz):
         ok = None
@@ -385,36 +386,56 @@
     shift_square = shift_turn * shift_turn
     upper = lax.broadcasted_iota(jnp.int32, (8, LANES), 0) < 4
 
+    def inverses(wide, scale):
+        diag_a, diag_b = wide + shift_a, wide + shift_b
+        scale_a = scale / (diag_a * diag_a + shift_square)
+        scale_b = scale / (diag_b * diag_b + shift_square)
+        return diag_a * scale_a, diag_b * scale_b, shift_turn * scale_a
+
     def spread(g, carry):
-        for side in range(2):
-            both = [
-                [
-                    u_a[pl.ds(pl.multiple_of((side * 6 + number) * ext + half + 8 * g, 8), 8), :]
-                    for half in (0, pairs)
-                ]
-                for number in range(6)
+        both = [
+            [
+                u_a[pl.ds(pl.multiple_of(number * ext + half + 8 * g, 8), 8), :]
+                for half in (0, pairs)
             ]
-            for i in range(8):
-                at = pl.ds(pl.multiple_of(64 * g + 8 * i, 8), 8)
-                wide = [
-                    jnp.where(
-                        upper,
-                        jnp.broadcast_to(first[i : i + 1, :], (8, LANES)),
-                        jnp.broadcast_to(second[i : i + 1, :], (8, LANES)),
-                    )
-                    for first, second in both
-                ]
-                for number in range(4):
-                    coef[side * 4 + number, at, :] = wide[number]
-                diag_a, diag_b = wide[4] + shift_a, wide[4] + shift_b
-                scale_a = wide[5] / (diag_a * diag_a + shift_square)
-                scale_b = wide[5] / (diag_b * diag_b + shift_square)
-                inv[side * 3, at, :] = diag_a * scale_a
-                inv[side * 3 + 1, at, :] = diag_b * scale_b
-                inv[side * 3 + 2, at, :] = shift_turn * scale_a
+            for number in range(6)
+        ]
+        for i in range(8):
+            at = pl.ds(pl.multiple_of(64 * g + 8 * i, 8), 8)
+            wide = [
+                jnp.where(
+                    upper,
+                    jnp.broadcast_to(first[i : i + 1, :], (8, LANES)),
+                    jnp.broadcast_to(second[i : i + 1, :], (8, LANES)),
+                )
+                for first, second in both
+            ]
+            for number in range(4):
+                coef[number, at, :] = wide[number]
+            for number, value in enumerate(inverses(wide[4], wide[5])):
+                inv[number, at, :] = value
         return carry
 
     lax.fori_loop(0, pairs // 8, spread, 0)
+
+    for jj in range(packs):
+        wide = []
+        for number in range(6):
+            total = jnp.zeros((8, LANES), jnp.float32)
+            for m in range(8):
+                row = (6 + number) * ext + jj + packs * m
+                line = jnp.where(
+                    upper,
+                    jnp.broadcast_to(u_a[pl.ds(row, 1), :], (8, LANES)),
+                    jnp.broadcast_to(u_a[pl.ds(row + pairs, 1), :], (8, LANES)),
+                )
+                total = jnp.where(lane // 16 == m, pltpu.roll(line, (16 * m + 8) % LANES, 1), total)
+            wide.append(total)
+        at = pl.ds(8 * jj, 8)
+        for number in range(4):
+            coef_s[number, at, :] = wide[number]
+        for number, value in enumerate(inverses(wide[4], wide[5])):
+            inv_s[number, at, :] = value
 
     own_rhs.wait()
     for d in range(1, 8):
@@ -481,77 +502,96 @@
         both = jnp.where(lane % 16 < 8, from_left[tile, :], from_right[tile, :])
         for f in range(8):
             at = strided(8 * g, f, 0)
-            rhs_f[2 + f // 4, at, :] = pltpu.roll(both, 120 - 16 * f, 1)
+            side_a[f // 4, at, :] = pltpu.roll(both, 120 - 16 * f, 1)
             if g == 0:
                 rhs_f[f // 4, at, :] = row_in_f[0, f]
             if g == ext // 8 - 1:
                 rhs_f[f // 4, at, :] = row_in_f[1, f]
 
-    def close(ref):
-        for which in range(4):
-            ref[which, pl.ds(0, 8), :] = pltpu.roll(ref[which, pl.ds(8 * pairs, 8), :], 4, 0)
-            ref[which, pl.ds(8 * pairs + 8, 8), :] = pltpu.roll(ref[which, pl.ds(8, 8), :], 4, 0)
-
-    chunk = pairs // 2
-
-    def begin(g, carry):
-        for i in range(chunk):
-            at = pl.ds(pl.multiple_of(8 * chunk * g + 8 * i, 8), 8)
-            mid = pl.ds(pl.multiple_of(8 * chunk * g + 8 * i + 8, 8), 8)
-            for side in range(2):
-                a, b = rhs_f[2 * side, at, :], rhs_f[2 * side + 1, at, :]
-                turn = inv[3 * side + 2, at, :]
-                v_a[2 * side, mid, :] = weights[0] * (inv[3 * side, at, :] * a + turn * b)
-                v_a[2 * side + 1, mid, :] = weights[0] * (inv[3 * side + 1, at, :] * b - turn * a)
-        return carry
-
-    lax.fori_loop(0, 2, begin, 0)
-    close(v_a)
-
-    def step(old, new, weight, last):
-        def body(g, carry):
-            def tile_of(which, i):
-                return old[which, pl.ds(pl.multiple_of(8 * chunk * g + 8 * i, 8), 8), :]
-
-            before = [tile_of(which, 0) for which in range(4)]
-            here = [tile_of(which, 1) for which in range(4)]
-            for i in range(chunk):
-                at = pl.ds(pl.multiple_of(8 * chunk * g + 8 * i, 8), 8)
-                mid = pl.ds(pl.multiple_of(8 * chunk * g + 8 * i + 8, 8), 8)
-                after = [tile_of(which, i + 2) for which in range(4)]
-                ups = [pltpu.roll(x, LANES - 1, 1) for x in here]
-                downs = [pltpu.roll(x, 1, 1) for x in here]
-                for side in range(1 if last else 2):
-                    north, south, east, west = [coef[4 * side + n, at, :] for n in range(4)]
-                    totals = []
-                    for part in range(2):
-                        own, other = 2 * side + part, 2 * (1 - side) + part
-                        right = jnp.where(lane == LANES - 1, ups[other], ups[own])
-                        left = jnp.where(lane == 0, downs[other], downs[own])
-                        totals.append(
-                            (rhs_f[own, at, :] + north * after[own])
-                            + (south * before[own] + east * right)
-                            + west * left
-                        )
-                    turn = inv[3 * side + 2, at, :]
-                    changes = (
-                        inv[3 * side, at, :] * totals[0] + turn * totals[1],
-                        inv[3 * side + 1, at, :] * totals[1] - turn * totals[0],
-                    )
-                    for part in range(2):
-                        own = 2 * side + part
-                        new[own, mid, :] = (1.0 - weight) * here[own] + weight * changes[part]
-                before, here = here, after
-            return carry
-
-        lax.fori_loop(0, 2, body, 0)
+    for part in range(2):
+        for jj in range(packs):
+            total = jnp.zeros((8, LANES), jnp.float32)
+            for m in range(8):
+                line = side_a[part, pl.ds(8 * (jj + packs * m), 8), :]
+                total = jnp.where(lane // 16 == m, pltpu.roll(line, (16 * m + 8) % LANES, 1), total)
+            side_f[part, pl.ds(8 * jj, 8), :] = total
+
+    def close(ref, side):
+        for part in range(2):
+            first = ref[part, pl.ds(8, 8), :]
+            final = ref[part, pl.ds(8 * pairs, 8), :]
+            ref[part, pl.ds(0, 8), :] = pltpu.roll(final, 4, 0)
+            ref[part, pl.ds(8 * pairs + 8, 8), :] = pltpu.roll(first, 4, 0)
+            first = side[part, pl.ds(8, 8), :]
+            final = side[part, pl.ds(8 * packs, 8), :]
+            first = jnp.where(lane < 16, pltpu.roll(first, 4, 0), first)
+            final = jnp.where(lane >= 112, pltpu.roll(final, 4, 0), final)
+            side[part, pl.ds(0, 8), :] = pltpu.roll(final, 16, 1)
+            side[part, pl.ds(8 * packs + 8, 8), :] = pltpu.roll(first, 112, 1)
+
+    def corrected(totals, inv_ref, at):
+        turn = inv_ref[2, at, :]
+        return (
+            inv_ref[0, at, :] * totals[0] + turn * totals[1],
+            inv_ref[1, at, :] * totals[1] - turn * totals[0],
+        )
+
+    def begin(count, right, inv_ref, new):
+        for j in range(count):
+            at, mid = pl.ds(8 * j, 8), pl.ds(8 * j + 8, 8)
+            changes = corrected([right[part, at, :] for part in range(2)], inv_ref, at)
+            for part in range(2):
+                new[part, mid, :] = weights[0] * changes[part]
+
+    def update(j, right, coef_ref, inv_ref, old, new, rights, lefts, weight):
+        at, mid, after = (pl.ds(8 * j + 8 * k, 8) for k in range(3))
+        north, south, east, west = [coef_ref[n, at, :] for n in range(4)]
+        totals = [
+            (right[part, at, :] + north * old[part, after, :])
+            + (south * old[part, at, :] + east * rights[part])
+            + west * lefts[part]
+            for part in range(2)
+        ]
+        changes = corrected(totals, inv_ref, at)
+        for part in range(2):
+            new[part, mid, :] = (1.0 - weight) * old[part, mid, :] + weight * changes[part]
+
+    def step(old, old_s, new, new_s, weight, last):
+        for jj in range(packs):
+            edges = [old_s[part, pl.ds(8 * jj + 8, 8), :] for part in range(2)]
+            inner = list(edges)
+            for m in range(8):
+                j = jj + packs * m
+                rights, lefts = [], []
+                for part in range(2):
+                    here = old[part, pl.ds(8 * j + 8, 8), :]
+                    outer = pltpu.roll(edges[part], 120 - 16 * m, 1)
+                    rights.append(pltpu.roll(jnp.where(lane == 0, outer, here), LANES - 1, 1))
+                    lefts.append(pltpu.roll(jnp.where(lane == LANES - 1, outer, here), 1, 1))
+                    if not last:
+                        moved = pltpu.roll(here, (16 * m + 8) % LANES, 1)
+                        inner[part] = jnp.where(lane // 16 == m, moved, inner[part])
+                update(j, rhs_f, coef, inv, old, new, rights, lefts, weight)
+            if not last:
+                rights = [
+                    pltpu.roll(jnp.where(lane % 16 == 8, inner[part], edges[part]), LANES - 1, 1)
+                    for part in range(2)
+                ]
+                lefts = [
+                    pltpu.roll(jnp.where(lane % 16 == 7, inner[part], edges[part]), 1, 1)
+                    for part in range(2)
+                ]
+                update(jj, side_f, coef_s, inv_s, old_s, new_s, rights, lefts, weight)
         if not last:
-            close(new)
-
-    old, new = v_a, v_b
+            close(new, new_s)
+
+    begin(pairs, rhs_f, inv, v_a)
+    begin(packs, side_f, inv_s, side_b)
+    close(v_a, side_b)
+    old, old_s, new, new_s = v_a, side_b, v_b, side_a
     for number in range(1, len(weights)):
-        step(old, new, weights[number], number == len(weights) - 1)
-        old, new = new, old
+        step(old, old_s, new, new_s, weights[number], number == len(weights) - 1)
+        old, old_s, new, new_s = new, new_s, old, old_s
 
     for g in range(groups):
         tile = pl.ds(8 * g, 8)
@@ -611,17 +651,22 @@
         functools.partial(patch_kernel, rows, row_count),
         out_shape=jax.ShapeDtypeStruct((rows, width), f32),
         in_specs=[pl.BlockSpec(memory_space=pl.ANY)] * 2,
-        out_specs=pl.BlockSpec(memory_space=pltpu.VMEM),
+        out_specs=pl.BlockSpec(memory_space=pl.ANY),
         scratch_shapes=[
             pltpu.VMEM((8, rows, LANES), f32),
             pltpu.VMEM((8, rows, LANES), f32),
             pltpu.VMEM((ext, width), f32),
+            pltpu.VMEM((2, 4 * ext, LANES), f32),
+            pltpu.VMEM((2, 4 * (ext + 4), LANES), f32),
+            pltpu.VMEM((2, 4 * (ext + 4), LANES), f32),
+            pltpu.VMEM((12 * ext, LANES), f32),
             pltpu.VMEM((4, 4 * ext, LANES), f32),
-            pltpu.VMEM((4, 4 * (ext + 4), LANES), f32),
-            pltpu.VMEM((4, 4 * (ext + 4), LANES), f32),
-            pltpu.VMEM((12 * ext, LANES), f32),
-            pltpu.VMEM((8, 4 * ext, LANES), f32),
-            pltpu.VMEM((6, 4 * ext, LANES), f32),
+            pltpu.VMEM((3, 4 * ext, LANES), f32),
+            pltpu.VMEM((2, ext // 2, LANES), f32),
+            pltpu.VMEM((2, 4 * ext, LANES), f32),
+            pltpu.VMEM((2, ext // 2 + 16, LANES), f32),
+            pltpu.VMEM((4, ext // 2, LANES), f32),
+            pltpu.VMEM((3, ext // 2, LANES), f32),
             pltpu.VMEM((rows, LANES), f32),
             pltpu.VMEM((ext, LANES), f32),
             pltpu.VMEM((ext, LANES), f32),

time: 24 us -> 56.4 us (2.35)
  Pallas kernels: 22.2 us -> 54.5 us
    pallas_call x1, Pallas kernels: 22.2 us -> 54.5 us  [patch_body(): pl.pallas_call(functools.partial(patch_kernel, rows, row_count), out_shap...]
where the time goes in v3:
time: 56.4 us; the launch traced here: 56.2 us
  Pallas kernels  54.5 us (97%)
  local copies, waits for them, and re-layouts  1.67 us (3%)
    pallas_call x1, Pallas kernels, patch_body(): pl.pallas_call(functools.partial(patch_kernel, rows, row_count), out_shap...  54.5 us
    unnamed x1, local copies, waits for them, and re-layouts  1.67 us

profile of v3, /device:TPU:0, one launch (start us, length us, event | category | flops | bytes accessed | tf_op | source)
XLA Modules:
  0.0 56.2 jit_solution(14573160981304211278)
XLA Ops:
  0.0 54.5 %patch_solve.1 = f32[64,1024]{1,0:T(8,128)} custom-call(f32[64,1024]{1,0:T(8,128)} %bitcast.3, f32[64,1024]{1,0:T(8,128)} %kappa.1), custom_call_target="tpu_custom_call" | custom-call | tf_op jit(solution)/shard_map/patch_solve/pallas_call | solution.py:650
  54.6 1.7 %copy.4 = f32[1,64,1024]{2,1,0:T(8,128)} copy(f32[1,64,1024]{2,1,0:T(8,128)} %bitcast.2) | data formatting | bytes 524288

commit v4 on v3

--- a/solution.py
+++ b/solution.py
@@ -261,8 +261,8 @@
 
 def patch_kernel(
     rows, row_count, rhs, kappa, out,
-    arrived, leaving, kap, rhs_f, v_a, v_b, u_a,
-    coef, inv, side_f, side_a, side_b, coef_s, inv_s, packed, from_left, from_right, row_out, row_in_f,
+    arrived, leaving, kap, rhs_f, v, u_a,
+    coef, inv, side_f, spare, v_s, coef_s, inv_s, packed, from_left, from_right, fields, row_in_f,
     go_s, go_r, back_s, back_r, halo_s, halo_r, kap_s, kap_r, local,
 ):
     mesh_id = pl.DeviceIdType.MESH
@@ -385,6 +385,9 @@
     shift_a, shift_b, shift_turn = sublane_constants()
     shift_square = shift_turn * shift_turn
     upper = lax.broadcasted_iota(jnp.int32, (8, LANES), 0) < 4
+
+    def tile_at(index):
+        return pl.ds(pl.multiple_of(8 * index, 8), 8)
 
     def inverses(wide, scale):
         diag_a, diag_b = wide + shift_a, wide + shift_b
@@ -418,12 +421,12 @@
 
     lax.fori_loop(0, pairs // 8, spread, 0)
 
-    for jj in range(packs):
+    def spread_sides(jj, carry):
         wide = []
         for number in range(6):
             total = jnp.zeros((8, LANES), jnp.float32)
             for m in range(8):
-                row = (6 + number) * ext + jj + packs * m
+                row = (6 + number) * ext + packs * m + jj
                 line = jnp.where(
                     upper,
                     jnp.broadcast_to(u_a[pl.ds(row, 1), :], (8, LANES)),
@@ -431,11 +434,14 @@
                 )
                 total = jnp.where(lane // 16 == m, pltpu.roll(line, (16 * m + 8) % LANES, 1), total)
             wide.append(total)
-        at = pl.ds(8 * jj, 8)
+        at = tile_at(jj)
         for number in range(4):
             coef_s[number, at, :] = wide[number]
         for number, value in enumerate(inverses(wide[4], wide[5])):
             inv_s[number, at, :] = value
+        return carry
+
+    lax.fori_loop(0, packs, spread_sides, 0)
 
     own_rhs.wait()
     for d in range(1, 8):
@@ -443,27 +449,27 @@
 
     log_alpha = math.log(circulant_alpha)
 
-    def strided(row, f, pad):
-        half, pair = row // pairs, row % pairs
+    def strided(block, f, pad):
+        half, pair = lax.div(block, packs), 8 * lax.rem(block, packs)
         return pl.ds(8 * (pair + pad) + 4 * half + f % 4, 8, stride=8)
 
-    for g in range(groups):
-        tile = pl.ds(8 * g, 8)
+    def transform(g, carry):
+        tile = tile_at(g)
         steps = [arrived[t, tile, :] * math.exp(log_alpha * t / 8) for t in range(8)]
         edges = jnp.zeros((8, LANES), jnp.float32)
         for f, value in enumerate(forward_eight(steps)):
-            rhs_f[f // 4, strided(HALO + 8 * g, f, 0), :] = value
+            rhs_f[f // 4, strided(g + 1, f, 0), :] = value
             edges = jnp.where(lane // 16 == f, pltpu.roll(value, 8 + 16 * f, 1), edges)
-            if g == 0:
-                row_out[0, f] = value
-            if g == groups - 1:
-                row_out[1, f] = value
+            fields[g, f] = value
         packed[tile, :] = edges
+        return carry
+
+    lax.fori_loop(0, groups, transform, 0)
 
     def halo_copy(number):
         dp, dz = SIDES[number]
         if dp == 0:
-            source = row_out.at[0 if dz < 0 else 1]
+            source = fields.at[0 if dz < 0 else groups - 1]
         else:
             first, count = {0: (0, groups), -1: (0, 1), 1: (groups - 1, 1)}[dz]
             source = packed.at[pl.ds(8 * first, 8 * count)]
@@ -497,37 +503,46 @@
             target[...] = jnp.zeros(target.shape, jnp.float32)
 
     weights = step_weights(DEGREE) * SWEEPS
-    for g in range(ext // 8):
-        tile = pl.ds(8 * g, 8)
+    def place_rows(g, carry):
+        for f in range(8):
+            rhs_f[f // 4, strided(g * (groups + 1), f, 0), :] = row_in_f[g, f]
+        return carry
+
+    lax.fori_loop(0, 2, place_rows, 0)
+
+    def place_sides(g, carry):
+        tile = tile_at(g)
         both = jnp.where(lane % 16 < 8, from_left[tile, :], from_right[tile, :])
         for f in range(8):
-            at = strided(8 * g, f, 0)
-            side_a[f // 4, at, :] = pltpu.roll(both, 120 - 16 * f, 1)
-            if g == 0:
-                rhs_f[f // 4, at, :] = row_in_f[0, f]
-            if g == ext // 8 - 1:
-                rhs_f[f // 4, at, :] = row_in_f[1, f]
-
-    for part in range(2):
-        for jj in range(packs):
+            spare[f // 4, strided(g, f, 0), :] = pltpu.roll(both, 120 - 16 * f, 1)
+        return carry
+
+    lax.fori_loop(0, ext // 8, place_sides, 0)
+
+    def pack_sides(jj, carry):
+        for part in range(2):
             total = jnp.zeros((8, LANES), jnp.float32)
             for m in range(8):
-                line = side_a[part, pl.ds(8 * (jj + packs * m), 8), :]
+                line = spare[part, tile_at(jj + packs * m), :]
                 total = jnp.where(lane // 16 == m, pltpu.roll(line, (16 * m + 8) % LANES, 1), total)
-            side_f[part, pl.ds(8 * jj, 8), :] = total
-
-    def close(ref, side):
+            side_f[part, tile_at(jj), :] = total
+        return carry
+
+    lax.fori_loop(0, packs, pack_sides, 0)
+
+    def close(slot):
         for part in range(2):
-            first = ref[part, pl.ds(8, 8), :]
-            final = ref[part, pl.ds(8 * pairs, 8), :]
-            ref[part, pl.ds(0, 8), :] = pltpu.roll(final, 4, 0)
-            ref[part, pl.ds(8 * pairs + 8, 8), :] = pltpu.roll(first, 4, 0)
-            first = side[part, pl.ds(8, 8), :]
-            final = side[part, pl.ds(8 * packs, 8), :]
+            base = 2 * slot + part
+            first = v[base, pl.ds(8, 8), :]
+            final = v[base, pl.ds(8 * pairs, 8), :]
+            v[base, pl.ds(0, 8), :] = pltpu.roll(final, 4, 0)
+            v[base, pl.ds(8 * pairs + 8, 8), :] = pltpu.roll(first, 4, 0)
+            first = v_s[base, pl.ds(8, 8), :]
+            final = v_s[base, pl.ds(8 * packs, 8), :]
             first = jnp.where(lane < 16, pltpu.roll(first, 4, 0), first)
             final = jnp.where(lane >= 112, pltpu.roll(final, 4, 0), final)
-            side[part, pl.ds(0, 8), :] = pltpu.roll(final, 16, 1)
-            side[part, pl.ds(8 * packs + 8, 8), :] = pltpu.roll(first, 112, 1)
+            v_s[base, pl.ds(0, 8), :] = pltpu.roll(final, 16, 1)
+            v_s[base, pl.ds(8 * packs + 8, 8), :] = pltpu.roll(first, 112, 1)
 
     def corrected(totals, inv_ref, at):
         turn = inv_ref[2, at, :]
@@ -536,68 +551,80 @@
             inv_ref[1, at, :] * totals[1] - turn * totals[0],
         )
 
-    def begin(count, right, inv_ref, new):
-        for j in range(count):
-            at, mid = pl.ds(8 * j, 8), pl.ds(8 * j + 8, 8)
-            changes = corrected([right[part, at, :] for part in range(2)], inv_ref, at)
+    def begin(right, inv_ref, new):
+        def body(j, carry):
+            changes = corrected([right[part, tile_at(j), :] for part in range(2)], inv_ref, tile_at(j))
             for part in range(2):
-                new[part, mid, :] = weights[0] * changes[part]
-
-    def update(j, right, coef_ref, inv_ref, old, new, rights, lefts, weight):
-        at, mid, after = (pl.ds(8 * j + 8 * k, 8) for k in range(3))
+                new[part, tile_at(j + 1), :] = weights[0] * changes[part]
+            return carry
+
+        return body
+
+    def update(j, right, coef_ref, inv_ref, state, old, new, rights, lefts, weight):
+        at, mid, after = tile_at(j), tile_at(j + 1), tile_at(j + 2)
         north, south, east, west = [coef_ref[n, at, :] for n in range(4)]
         totals = [
-            (right[part, at, :] + north * old[part, after, :])
-            + (south * old[part, at, :] + east * rights[part])
+            (right[part, at, :] + north * state[old + part, after, :])
+            + (south * state[old + part, at, :] + east * rights[part])
             + west * lefts[part]
             for part in range(2)
         ]
         changes = corrected(totals, inv_ref, at)
         for part in range(2):
-            new[part, mid, :] = (1.0 - weight) * old[part, mid, :] + weight * changes[part]
-
-    def step(old, old_s, new, new_s, weight, last):
-        for jj in range(packs):
-            edges = [old_s[part, pl.ds(8 * jj + 8, 8), :] for part in range(2)]
+            kept = (1.0 - weight) * state[old + part, mid, :]
+            state[new + part, mid, :] = kept + weight * changes[part]
+
+    lax.fori_loop(0, pairs, begin(rhs_f, inv, v), 0, unroll=8)
+    lax.fori_loop(0, packs, begin(side_f, inv_s, v_s), 0, unroll=packs)
+    close(0)
+
+    def step(number, carry):
+        old = 2 * lax.rem(number + 1, 2)
+        new = 2 - old
+        which = lax.rem(number, DEGREE)
+        weight = jnp.float32(weights[0])
+        for at in range(1, DEGREE):
+            weight = jnp.where(which == at, jnp.float32(weights[at]), weight)
+
+        def group(jj, carry):
+            edges = [v_s[old + part, tile_at(jj + 1), :] for part in range(2)]
             inner = list(edges)
             for m in range(8):
                 j = jj + packs * m
                 rights, lefts = [], []
                 for part in range(2):
-                    here = old[part, pl.ds(8 * j + 8, 8), :]
+                    here = v[old + part, tile_at(j + 1), :]
                     outer = pltpu.roll(edges[part], 120 - 16 * m, 1)
                     rights.append(pltpu.roll(jnp.where(lane == 0, outer, here), LANES - 1, 1))
                     lefts.append(pltpu.roll(jnp.where(lane == LANES - 1, outer, here), 1, 1))
-                    if not last:
-                        moved = pltpu.roll(here, (16 * m + 8) % LANES, 1)
-                        inner[part] = jnp.where(lane // 16 == m, moved, inner[part])
-                update(j, rhs_f, coef, inv, old, new, rights, lefts, weight)
-            if not last:
-                rights = [
-                    pltpu.roll(jnp.where(lane % 16 == 8, inner[part], edges[part]), LANES - 1, 1)
-                    for part in range(2)
-                ]
-                lefts = [
-                    pltpu.roll(jnp.where(lane % 16 == 7, inner[part], edges[part]), 1, 1)
-                    for part in range(2)
-                ]
-                update(jj, side_f, coef_s, inv_s, old_s, new_s, rights, lefts, weight)
-        if not last:
-            close(new, new_s)
-
-    begin(pairs, rhs_f, inv, v_a)
-    begin(packs, side_f, inv_s, side_b)
-    close(v_a, side_b)
-    old, old_s, new, new_s = v_a, side_b, v_b, side_a
-    for number in range(1, len(weights)):
-        step(old, old_s, new, new_s, weights[number], number == len(weights) - 1)
-        old, old_s, new, new_s = new, new_s, old, old_s
-
-    for g in range(groups):
-        tile = pl.ds(8 * g, 8)
-        fields = [old[f // 4, strided(HALO + 8 * g, f, 1), :] for f in range(8)]
-        for t, value in enumerate(backward_eight(fields)):
-            leaving[t, tile, :] = value * (math.exp(-log_alpha * t / 8) / 8)
+                    moved = pltpu.roll(here, (16 * m + 8) % LANES, 1)
+                    inner[part] = jnp.where(lane // 16 == m, moved, inner[part])
+                update(j, rhs_f, coef, inv, v, old, new, rights, lefts, weight)
+            rights = [
+                pltpu.roll(jnp.where(lane % 16 == 8, inner[part], edges[part]), LANES - 1, 1)
+                for part in range(2)
+            ]
+            lefts = [
+                pltpu.roll(jnp.where(lane % 16 == 7, inner[part], edges[part]), 1, 1)
+                for part in range(2)
+            ]
+            update(jj, side_f, coef_s, inv_s, v_s, old, new, rights, lefts, weight)
+            return carry
+
+        lax.fori_loop(0, packs, group, 0)
+        close(lax.div(new, 2))
+        return carry
+
+    lax.fori_loop(1, len(weights), step, 0)
+    final = 2 * ((len(weights) - 1) % 2)
+
+    def inverse(g, carry):
+        found = [v[final + f // 4, strided(g + 1, f, 1), :] for f in range(8)]
+        for t, value in enumerate(backward_eight(found)):
+            leaving[t, tile_at(g), :] = value * (math.exp(-log_alpha * t / 8) / 8)
+        return carry
+
+    lax.fori_loop(0, groups, inverse, 0)
 
     columns = pl.ds(pl.multiple_of(p * LANES, LANES), LANES)
 
@@ -657,20 +684,19 @@
             pltpu.VMEM((8, rows, LANES), f32),
             pltpu.VMEM((ext, width), f32),
             pltpu.VMEM((2, 4 * ext, LANES), f32),
-            pltpu.VMEM((2, 4 * (ext + 4), LANES), f32),
-            pltpu.VMEM((2, 4 * (ext + 4), LANES), f32),
+            pltpu.VMEM((4, 4 * (ext + 4), LANES), f32),
             pltpu.VMEM((12 * ext, LANES), f32),
             pltpu.VMEM((4, 4 * ext, LANES), f32),
             pltpu.VMEM((3, 4 * ext, LANES), f32),
             pltpu.VMEM((2, ext // 2, LANES), f32),
             pltpu.VMEM((2, 4 * ext, LANES), f32),
-            pltpu.VMEM((2, ext // 2 + 16, LANES), f32),
+            pltpu.VMEM((4, ext // 2 + 16, LANES), f32),
             pltpu.VMEM((4, ext // 2, LANES), f32),
             pltpu.VMEM((3, ext // 2, LANES), f32),
             pltpu.VMEM((rows, LANES), f32),
             pltpu.VMEM((ext, LANES), f32),
             pltpu.VMEM((ext, LANES), f32),
-            pltpu.VMEM((2, 8, HALO, LANES), f32),
+            pltpu.VMEM((rows // 8, 8, HALO, LANES), f32),
             pltpu.VMEM((2, 8, HALO, LANES), f32),
             dma((8,)), dma((8,)), dma((8,)), dma((8,)), dma((8,)), dma((8,)),
             dma((2,)), dma((2,)), dma((3,)),

time: 56.4 us -> 50 us (0.89)
  Pallas kernels: 54.5 us -> 48.2 us
    pallas_call x1, Pallas kernels: 54.5 us -> 48.2 us  [patch_body(): pl.pallas_call(functools.partial(patch_kernel, rows, row_count), out_shap...]
where the time goes in v4:
time: 50 us; the launch traced here: 49.8 us
  Pallas kernels  48.2 us (96%)
  local copies, waits for them, and re-layouts  1.67 us (3%)
    pallas_call x1, Pallas kernels, patch_body(): pl.pallas_call(functools.partial(patch_kernel, rows, row_count), out_shap...  48.2 us
    unnamed x1, local copies, waits for them, and re-layouts  1.67 us

profile of v4, /device:TPU:0, one launch (start us, length us, event | category | flops | bytes accessed | tf_op | source)
XLA Modules:
  0.0 49.8 jit_solution(3898454941107859860)
XLA Ops:
  0.0 48.2 %patch_solve.1 = f32[64,1024]{1,0:T(8,128)} custom-call(f32[64,1024]{1,0:T(8,128)} %bitcast.3, f32[64,1024]{1,0:T(8,128)} %kappa.1), custom_call_target="tpu_custom_call" | custom-call | tf_op jit(solution)/shard_map/patch_solve/pallas_call | solution.py:677
  48.2 1.7 %copy.4 = f32[1,64,1024]{2,1,0:T(8,128)} copy(f32[1,64,1024]{2,1,0:T(8,128)} %bitcast.2) | data formatting | bytes 524288

commit v5 on v4

--- a/solution.py
+++ b/solution.py
@@ -678,7 +678,7 @@
         functools.partial(patch_kernel, rows, row_count),
         out_shape=jax.ShapeDtypeStruct((rows, width), f32),
         in_specs=[pl.BlockSpec(memory_space=pl.ANY)] * 2,
-        out_specs=pl.BlockSpec(memory_space=pl.ANY),
+        out_specs=pl.BlockSpec(memory_space=pltpu.VMEM),
         scratch_shapes=[
             pltpu.VMEM((8, rows, LANES), f32),
             pltpu.VMEM((8, rows, LANES), f32),

time: 50 us -> 50.5 us (1.010)
    pallas_call x1, Pallas kernels: 48.2 us -> 48.7 us  [patch_body(): pl.pallas_call(functools.partial(patch_kernel, rows, row_count), out_shap...]
where the time goes in v5:
time: 50.5 us; the launch traced here: 50.4 us
  Pallas kernels  48.7 us (96%)
  local copies, waits for them, and re-layouts  1.67 us (3%)
    pallas_call x1, Pallas kernels, patch_body(): pl.pallas_call(functools.partial(patch_kernel, rows, row_count), out_shap...  48.7 us
    unnamed x1, local copies, waits for them, and re-layouts  1.67 us

profile of v5, /device:TPU:0, one launch (start us, length us, event | category | flops | bytes accessed | tf_op | source)
XLA Modules:
  0.0 50.4 jit_solution(12758768321494999576)
XLA Ops:
  0.0 48.7 %patch_solve.1 = f32[64,1024]{1,0:T(8,128)} custom-call(f32[64,1024]{1,0:T(8,128)} %bitcast.3, f32[64,1024]{1,0:T(8,128)} %kappa.1), custom_call_target="tpu_custom_call" | custom-call | tf_op jit(solution)/shard_map/patch_solve/pallas_call | solution.py:677
  48.7 1.7 %copy.4 = f32[1,64,1024]{2,1,0:T(8,128)} copy(f32[1,64,1024]{2,1,0:T(8,128)} %bitcast.2) | data formatting | bytes 524288

commit v6 on v5

--- a/solution.py
+++ b/solution.py
@@ -221,7 +221,7 @@
 
 
 def sublane_constants():
-    field = lax.broadcasted_iota(jnp.int32, (8, LANES), 0) % 4
+    field = lax.broadcasted_iota(jnp.int32, (8, LANES), 0) & 3
     decay = circulant_alpha ** (1.0 / 8)
     real = jnp.zeros((8, LANES), jnp.float32)
     turn = jnp.zeros((8, LANES), jnp.float32)
@@ -355,6 +355,7 @@
             kap[pl.ds(lost, HALO), :] = jnp.zeros((HALO, kap.shape[1]), jnp.float32)
 
     lane = lax.broadcasted_iota(jnp.int32, (8, LANES), 1)
+    lane_group, lane_place = lane & 112, lane & 15
     lane_all = lax.broadcasted_iota(jnp.int32, (ext, LANES), 1)
 
     def kap_block(which):
@@ -432,7 +433,7 @@
                     jnp.broadcast_to(u_a[pl.ds(row, 1), :], (8, LANES)),
                     jnp.broadcast_to(u_a[pl.ds(row + pairs, 1), :], (8, LANES)),
                 )
-                total = jnp.where(lane // 16 == m, pltpu.roll(line, (16 * m + 8) % LANES, 1), total)
+                total = jnp.where(lane_group == 16 * m, pltpu.roll(line, (16 * m + 8) % LANES, 1), total)
             wide.append(total)
         at = tile_at(jj)
         for number in range(4):
@@ -459,7 +460,7 @@
         edges = jnp.zeros((8, LANES), jnp.float32)
         for f, value in enumerate(forward_eight(steps)):
             rhs_f[f // 4, strided(g + 1, f, 0), :] = value
-            edges = jnp.where(lane // 16 == f, pltpu.roll(value, 8 + 16 * f, 1), edges)
+            edges = jnp.where(lane_group == 16 * f, pltpu.roll(value, 8 + 16 * f, 1), edges)
             fields[g, f] = value
         packed[tile, :] = edges
         return carry
@@ -512,7 +513,7 @@
 
     def place_sides(g, carry):
         tile = tile_at(g)
-        both = jnp.where(lane % 16 < 8, from_left[tile, :], from_right[tile, :])
+        both = jnp.where(lane_place < 8, from_left[tile, :], from_right[tile, :])
         for f in range(8):
             spare[f // 4, strided(g, f, 0), :] = pltpu.roll(both, 120 - 16 * f, 1)
         return carry
@@ -524,7 +525,7 @@
             total = jnp.zeros((8, LANES), jnp.float32)
             for m in range(8):
                 line = spare[part, tile_at(jj + packs * m), :]
-                total = jnp.where(lane // 16 == m, pltpu.roll(line, (16 * m + 8) % LANES, 1), total)
+                total = jnp.where(lane_group == 16 * m, pltpu.roll(line, (16 * m + 8) % LANES, 1), total)
             side_f[part, tile_at(jj), :] = total
         return carry
 
@@ -598,14 +599,14 @@
                     rights.append(pltpu.roll(jnp.where(lane == 0, outer, here), LANES - 1, 1))
                     lefts.append(pltpu.roll(jnp.where(lane == LANES - 1, outer, here), 1, 1))
                     moved = pltpu.roll(here, (16 * m + 8) % LANES, 1)
-                    inner[part] = jnp.where(lane // 16 == m, moved, inner[part])
+                    inner[part] = jnp.where(lane_group == 16 * m, moved, inner[part])
                 update(j, rhs_f, coef, inv, v, old, new, rights, lefts, weight)
             rights = [
-                pltpu.roll(jnp.where(lane % 16 == 8, inner[part], edges[part]), LANES - 1, 1)
+                pltpu.roll(jnp.where(lane_place == 8, inner[part], edges[part]), LANES - 1, 1)
                 for part in range(2)
             ]
             lefts = [
-                pltpu.roll(jnp.where(lane % 16 == 7, inner[part], edges[part]), 1, 1)
+                pltpu.roll(jnp.where(lane_place == 7, inner[part], edges[part]), 1, 1)
                 for part in range(2)
             ]
             update(jj, side_f, coef_s, inv_s, v_s, old, new, rights, lefts, weight)

time: 50.5 us -> 50.6 us (level)
  no operation moved by 1% of the time
where the time goes in v6:
time: 50.6 us; the launch traced here: 50.4 us
  Pallas kernels  48.7 us (96%)
  local copies, waits for them, and re-layouts  1.67 us (3%)
    pallas_call x1, Pallas kernels, patch_body(): pl.pallas_call(functools.partial(patch_kernel, rows, row_count), out_shap...  48.7 us
    unnamed x1, local copies, waits for them, and re-layouts  1.67 us

profile of v6, /device:TPU:0, one launch (start us, length us, event | category | flops | bytes accessed | tf_op | source)
XLA Modules:
  0.0 50.4 jit_solution(12961608572830682373)
XLA Ops:
  0.0 48.7 %patch_solve.1 = f32[64,1024]{1,0:T(8,128)} custom-call(f32[64,1024]{1,0:T(8,128)} %bitcast.3, f32[64,1024]{1,0:T(8,128)} %kappa.1), custom_call_target="tpu_custom_call" | custom-call | tf_op jit(solution)/shard_map/patch_solve/pallas_call | solution.py:678
  48.8 1.7 %copy.4 = f32[1,64,1024]{2,1,0:T(8,128)} copy(f32[1,64,1024]{2,1,0:T(8,128)} %bitcast.2) | data formatting | bytes 524288

commit v7 on v2

--- a/solution.py
+++ b/solution.py
@@ -354,6 +354,7 @@
             kap[pl.ds(lost, HALO), :] = jnp.zeros((HALO, kap.shape[1]), jnp.float32)
 
     lane = lax.broadcasted_iota(jnp.int32, (8, LANES), 1)
+    lane_group, lane_place = lane & 112, lane & 15
     lane_all = lax.broadcasted_iota(jnp.int32, (ext, LANES), 1)
 
     def kap_block(which):
@@ -432,7 +433,7 @@
         edges = jnp.zeros((8, LANES), jnp.float32)
         for f, value in enumerate(forward_eight(steps)):
             rhs_f[f // 4, strided(HALO + 8 * g, f, 0), :] = value
-            edges = jnp.where(lane // 16 == f, pltpu.roll(value, 8 + 16 * f, 1), edges)
+            edges = jnp.where(lane_group == 16 * f, pltpu.roll(value, 8 + 16 * f, 1), edges)
             if g == 0:
                 row_out[0, f] = value
             if g == groups - 1:
@@ -478,7 +479,7 @@
     weights = step_weights(DEGREE) * SWEEPS
     for g in range(ext // 8):
         tile = pl.ds(8 * g, 8)
-        both = jnp.where(lane % 16 < 8, from_left[tile, :], from_right[tile, :])
+        both = jnp.where(lane_place < 8, from_left[tile, :], from_right[tile, :])
         for f in range(8):
             at = strided(8 * g, f, 0)
             rhs_f[2 + f // 4, at, :] = pltpu.roll(both, 120 - 16 * f, 1)
@@ -548,10 +549,21 @@
         if not last:
             close(new)
 
-    old, new = v_a, v_b
-    for number in range(1, len(weights)):
-        step(old, new, weights[number], number == len(weights) - 1)
-        old, new = new, old
+    def weight_at(number):
+        which = lax.rem(number, DEGREE)
+        weight = jnp.float32(weights[0])
+        for at in range(1, DEGREE):
+            weight = jnp.where(which == at, jnp.float32(weights[at]), weight)
+        return weight
+
+    def two_steps(number, carry):
+        step(v_a, v_b, weight_at(2 * number + 1), False)
+        step(v_b, v_a, weight_at(2 * number + 2), False)
+        return carry
+
+    lax.fori_loop(0, len(weights) // 2 - 1, two_steps, 0)
+    step(v_a, v_b, weights[-1], True)
+    old = v_b
 
     for g in range(groups):
         tile = pl.ds(8 * g, 8)

time: 24 us -> 24 us (level)
  no operation moved by 1% of the time
where the time goes in v7:
time: 24 us; the launch traced here: 23.9 us
  Pallas kernels  22.2 us (92%)
  local copies, waits for them, and re-layouts  1.67 us (7%)
    pallas_call x1, Pallas kernels, patch_body(): pl.pallas_call(functools.partial(patch_kernel, rows, row_count), out_shap...  22.2 us
    unnamed x1, local copies, waits for them, and re-layouts  1.67 us

profile of v7, /device:TPU:0, one launch (start us, length us, event | category | flops | bytes accessed | tf_op | source)
XLA Modules:
  0.0 23.9 jit_solution(3117467184654319491)
XLA Ops:
  0.0 22.2 %patch_solve.1 = f32[64,1024]{1,0:T(8,128)} custom-call(f32[64,1024]{1,0:T(8,128)} %bitcast.3, f32[64,1024]{1,0:T(8,128)} %kappa.1), custom_call_target="tpu_custom_call" | custom-call | tf_op jit(solution)/shard_map/patch_solve/pallas_call | solution.py:622
  22.2 1.7 %copy.4 = f32[1,64,1024]{2,1,0:T(8,128)} copy(f32[1,64,1024]{2,1,0:T(8,128)} %bitcast.2) | data formatting | bytes 524288
